TPU v7x, 128 devices: a whole 4x4x4 slice. The times are simulated.
128 devices in a mesh: prow: 8 (over z, core), pcol: 16 (over y, x).
Axes of the slice: x: 4, y: 4, z: 4, core: 2. Of those that a mesh axis runs over, the one named last changes fastest.
Arguments:
- matrix: float32 [20480, 20480], P('prow', 'pcol'), may hold values from -40 to 40, as said below
Outputs:
- factored: float32 [20480, 20480], P('prow', 'pcol')
Inputs may be any that keep to these rules, and one draw needn't show every extreme that they name: `matrix`: A is symmetric and positive definite.
All inputs are finite; a program needn't handle non-finite values.
Results may differ from a plain program's by a relative error of at most 0.0003.
Values sent between devices are 32-bit elements; how exact they have to be, the bound alone decides.
A program may use at most 128 MiB of HBM per device.

v0:
```python
import jax
import jax.numpy as jnp
from jax import lax
from jax.sharding import PartitionSpec as P

NB = 256


def spread(block, axis, source):
    block = jnp.where(lax.axis_index(axis) == source, block, jnp.zeros_like(block))
    return lax.psum(block, axis)


def outer_update(row_panel, col_panel):
    return lax.dot_general(
        row_panel,
        col_panel,
        (((1,), (1,)), ((), ())),
        precision=lax.Precision.HIGHEST,
        preferred_element_type=jnp.float32,
    )


def solve_panel(diagonal, column, row_global, panel_index, my_row):
    lower_factor = jnp.tril(jnp.linalg.cholesky(diagonal))
    solved = jax.scipy.linalg.solve_triangular(lower_factor, column.T, lower=True).T
    row_panel = jnp.where((row_global > panel_index)[:, None], solved, jnp.zeros_like(solved))
    first_rows = jnp.where(my_row == panel_index, lower_factor, row_panel[:NB])
    return row_panel.at[:NB].set(first_rows)


def factor(column, panel_index, row_global, my_row, my_col, row_count, col_count):
    diagonal = spread(column[:NB], "prow", panel_index % row_count)
    row_panel = solve_panel(diagonal, column, row_global, panel_index, my_row)
    row_panel = spread(row_panel, "pcol", panel_index % col_count)
    group_ratio = col_count // row_count
    local_cols = row_panel.shape[0] // (NB * group_ratio)
    grouped = row_panel.reshape(local_cols, group_ratio * NB, NB)
    chosen = lax.dynamic_slice_in_dim(grouped, my_col // row_count * NB, NB, 1)
    chosen = chosen.reshape(local_cols * NB, NB)
    col_panel = spread(chosen, "prow", my_col % row_count)
    return (row_panel, col_panel)


def finish(updated, row_panel, panel_index, row_global, col_global, my_col):
    zeroed = jnp.logical_and(
        (row_global == panel_index)[:, None], (col_global > panel_index)[None, :]
    )
    updated = jnp.where(zeroed, jnp.zeros_like(updated), updated)
    first_cols = jnp.where(my_col == panel_index, row_panel, updated[:, :NB])
    return updated.at[:, :NB].set(first_cols)


def body(matrix):
    row_count = lax.axis_size("prow")
    col_count = lax.axis_size("pcol")
    my_row = lax.axis_index("prow")
    my_col = lax.axis_index("pcol")
    local_rows, local_width = matrix.shape
    row_global = jnp.arange(local_rows, dtype=jnp.int32) // NB * row_count + my_row
    col_global = jnp.arange(local_width, dtype=jnp.int32) // NB * col_count + my_col
    for panel_index in range(2):
        row_panel, col_panel = factor(
            matrix[:, :NB], panel_index, row_global, my_row, my_col, row_count, col_count
        )
        updated = matrix - outer_update(row_panel, col_panel)
        matrix = finish(updated, row_panel, panel_index, row_global, col_global, my_col)
    return matrix


def solution(mesh):
    in_specs = (P("prow", "pcol"),)
    out_specs = P("prow", "pcol")
    return jax.shard_map(body, mesh=mesh, in_specs=in_specs, out_specs=out_specs, check_vma=False)
```

profile of v0, /device:TPU:0, one launch (start us, length us, event | category | flops | bytes accessed | tf_op | source)
XLA Modules:
  0.0 669.3 jit_solution(8243354790649346700)
XLA Ops:
  6.5 13.9 %copy.24 = f32[2560,1280]{0,1:T(8,128)} copy(f32[2560,1280]{1,0:T(8,128)} %param.12) | data formatting | bytes 26214400 | tf_op args[0]
  20.4 1.7 slice_select_fusion.3
  22.2 1.9 slice_bitcast_fusion
  24.1 60.7 %all-reduce.8.cloned.1.call-done = f32[256,256]{0,1:T(8,128)} async-done(((f32[256,256]{0,1:T(8,128)}), f32[256,256]{0,1:T(8,128)}) %all-reduce.8.cloned.1.call-update) | async-done | bytes 262160 | tf_op jit(solution)/shard_map/psum | solution.py:11
  84.8 1.1 copy.18
  85.9 1.0 fusion.12
  86.9 11.7 %cholesky.130 = f32[128,128]{1,0:T(8,128)S(1)} custom-call(f32[128,128]{1,0:T(8,128)S(1)} %cholesky.194), custom_call_target="Cholesky" | custom-call | tf_op jit(solution)/shard_map/jit(cholesky)/cholesky | solution.py:25
  98.6 9.8 %custom-call.13 = f32[1,128,128]{1,2,0:T(8,128)S(1)} custom-call(f32[1,128,128]{2,1,0:T(8,128)S(1)} %get-tuple-element.112), custom_call_target="InvertDiagBlocksLowerTriangular" | custom-call | tf_op jit(solution)/shard_map/jit(cholesky)/cholesky | solution.py:25
  108.9 11.7 %cholesky.147 = f32[128,128]{1,0:T(8,128)S(1)} custom-call(f32[128,128]{1,0:T(8,128)S(1)} %convolution_subtract_fusion.5), custom_call_target="Cholesky" | custom-call | tf_op jit(solution)/shard_map/jit(cholesky)/cholesky | solution.py:25
  121.0 0.7 compare_reduce_fusion.2
  123.2 4.5 while.8
  124.0 1.3 dynamic-slice.44
  126.2 1.3 dynamic-slice.44
  127.6 19.7 %custom-call.14 = f32[2,128,128]{1,2,0:T(8,128)S(1)} custom-call(f32[2,128,128]{2,1,0:T(8,128)S(1)} %get-tuple-element.69), custom_call_target="InvertDiagBlocksLowerTriangular" | custom-call | tf_op jit(solution)/shard_map/jit(_solve_triangular)/triangular_solve | solution.py:26
  147.3 1.3 fusion.7
  148.6 2.3 convolution_subtract_fusion.3
  150.9 1.3 fusion.20
  152.5 1.7 broadcast_select_fusion.1
  154.3 91.7 %all-reduce.10.cloned.1.call-done = f32[2560,256]{0,1:T(8,128)} async-done(((f32[2560,256]{0,1:T(8,128)}), f32[2560,256]{0,1:T(8,128)}) %all-reduce.10.cloned.1.call-update) | async-done | bytes 2621456 | tf_op jit(solution)/shard_map/psum | solution.py:11
  246.0 3.3 copy.23
  249.2 2.7 dynamic-slice_select_fusion.1
  252.7 62.3 %all-reduce.12.cloned.1.call-done = f32[1280,256]{1,0:T(8,128)} async-done(((f32[1280,256]{1,0:T(8,128)}), f32[1280,256]{1,0:T(8,128)}) %all-reduce.12.cloned.1.call-update) | async-done | bytes 1310736 | tf_op jit(solution)/shard_map/psum | solution.py:11
  315.0 16.4 %fusion.1 = f32[2560,1280]{0,1:T(8,128)} fusion(f32[2560,1280]{0,1:T(8,128)} %copy.24, f32[2560,256]{0,1:T(8,128)S(1)} %copy-done, f32[1280,256]{1,0:T(8,128)} %all-reduce.12.cloned.1.call-done, pred[2560]{0:T(1024)(128)(4,1)S(1)} %fusion.31, pred[1280]{0:T(1024)(128)(4,1)S(1)} %fusion.38), kind=kOutput, calls=%fused_computation.7 | convolution fusion | flops 10076160000 | bytes 30150400 | tf_op jit(solution)/shard_map/dot_general | solution.py:15
  331.4 4.3 constant_dynamic-update-slice_fusion.2
  335.7 1.5 copy-done.2
  337.2 0.7 slice_select_fusion.1
  338.3 59.1 %all-reduce.14.cloned.1.call-done = f32[256,256]{0,1:T(8,128)} async-done(((f32[256,256]{0,1:T(8,128)}), f32[256,256]{0,1:T(8,128)}) %all-reduce.14.cloned.1.call-update) | async-done | bytes 262160 | tf_op jit(solution)/shard_map/psum | solution.py:11
  397.4 1.1 copy.26
  398.5 1.1 fusion.11
  399.7 11.7 %cholesky.164 = f32[128,128]{1,0:T(8,128)S(1)} custom-call(f32[128,128]{1,0:T(8,128)S(1)} %cholesky.197), custom_call_target="Cholesky" | custom-call | tf_op jit(solution)/shard_map/jit(cholesky)/cholesky | solution.py:25
  411.4 9.8 %custom-call.15 = f32[1,128,128]{1,2,0:T(8,128)S(1)} custom-call(f32[1,128,128]{2,1,0:T(8,128)S(1)} %get-tuple-element.110), custom_call_target="InvertDiagBlocksLowerTriangular" | custom-call | tf_op jit(solution)/shard_map/jit(cholesky)/cholesky | solution.py:25
  421.7 11.7 %cholesky.181 = f32[128,128]{1,0:T(8,128)S(1)} custom-call(f32[128,128]{1,0:T(8,128)S(1)} %convolution_subtract_fusion.4), custom_call_target="Cholesky" | custom-call | tf_op jit(solution)/shard_map/jit(cholesky)/cholesky | solution.py:25
  433.8 0.7 compare_reduce_fusion
  436.5 4.4 while.9
  437.4 1.3 dynamic-slice.46
  439.4 1.3 dynamic-slice.46
  440.9 19.7 %custom-call.16 = f32[2,128,128]{1,2,0:T(8,128)S(1)} custom-call(f32[2,128,128]{2,1,0:T(8,128)S(1)} %get-tuple-element.70), custom_call_target="InvertDiagBlocksLowerTriangular" | custom-call | tf_op jit(solution)/shard_map/jit(_solve_triangular)/triangular_solve | solution.py:26
  460.6 1.3 fusion.5
  461.9 1.3 convolution_subtract_fusion.2
  463.1 1.3 fusion.16
  464.7 1.7 broadcast_select_fusion
  466.5 91.7 %all-reduce.16.cloned.1.call-done = f32[2560,256]{0,1:T(8,128)} async-done(((f32[2560,256]{0,1:T(8,128)}), f32[2560,256]{0,1:T(8,128)}) %all-reduce.16.cloned.1.call-update) | async-done | bytes 2621456 | tf_op jit(solution)/shard_map/psum | solution.py:11
  558.2 3.3 copy.31
  561.4 2.7 dynamic-slice_select_fusion
  564.2 63.1 %all-reduce.18.cloned.1.call-done = f32[1280,256]{1,0:T(8,128)} async-done(((f32[1280,256]{1,0:T(8,128)}), f32[1280,256]{1,0:T(8,128)}) %all-reduce.18.cloned.1.call-update) | async-done | bytes 1310736 | tf_op jit(solution)/shard_map/psum | solution.py:11
  627.2 16.6 %fusion = f32[2560,1280]{0,1:T(8,128)} fusion(f32[2560,1280]{0,1:T(8,128)} %get-tuple-element.103, f32[2560,256]{0,1:T(8,128)S(1)} %copy-done.1, f32[1280,256]{1,0:T(8,128)} %all-reduce.18.cloned.1.call-done, pred[2560]{0:T(1024)(128)(4,1)S(1)} %fusion.32, pred[1280]{0:T(1024)(128)(4,1)S(1)} %fusion.39), kind=kOutput, calls=%fused_computation.5 | convolution fusion | flops 10076160000 | bytes 30150400 | tf_op jit(solution)/shard_map/dot_general | solution.py:15
  643.8 4.3 fusion.2
  648.1 13.9 %copy.33 = f32[2560,1280]{1,0:T(8,128)} copy(f32[2560,1280]{0,1:T(8,128)} %fusion.2) | data formatting | bytes 26214400 | tf_op jit(solution)/shard_map/scatter | solution.py:51
  (75 shorter events, 7.3 us)
Async XLA Ops:
  6.5 78.3 %all-reduce.8.cloned.1.call-start = ((), (), s32[]{:S(2)}) async-start(), calls=%async_computation | async-start | bytes 524288 | tf_op jit(solution)/shard_map/psum | solution.py:11
  22.1 223.8 %all-reduce.10.cloned.1.call-start = ((), (), s32[]{:S(2)}) async-start(), calls=%async_computation.1 | async-start | bytes 5242880 | tf_op jit(solution)/shard_map/psum | solution.py:11
  154.2 160.8 %all-reduce.12.cloned.1.call-start = ((), (), s32[]{:S(2)}) async-start(), calls=%async_computation.2 | async-start | bytes 2621440 | tf_op jit(solution)/shard_map/psum | solution.py:11
  249.2 65.8 %copy-start = (f32[2560,256]{0,1:T(8,128)S(1)}, f32[2560,256]{0,1:T(8,128)}, u32[]{:S(2)}) copy-start(f32[2560,256]{0,1:T(8,128)} %all-reduce.10.cloned.1.call-done) | copy-start | bytes 7864324
  251.9 145.5 %all-reduce.14.cloned.1.call-start = ((), (), s32[]{:S(2)}) async-start(), calls=%async_computation.3 | async-start | bytes 524288 | tf_op jit(solution)/shard_map/psum | solution.py:11
  335.7 1.5 copy-start.2
  338.0 220.2 %all-reduce.16.cloned.1.call-start = ((), (), s32[]{:S(2)}) async-start(), calls=%async_computation.4 | async-start | bytes 5242880 | tf_op jit(solution)/shard_map/psum | solution.py:11
  398.5 62.1 %copy-start.3 = (f32[2560,256]{0,1:T(8,128)S(1)}, f32[2560,256]{0,1:T(8,128)}, u32[]{:S(2)}) copy-start(f32[2560,256]{0,1:T(8,128)} %copy-done.2) | copy-start | bytes 7864324
  466.4 160.8 %all-reduce.18.cloned.1.call-start = ((), (), s32[]{:S(2)}) async-start(), calls=%async_computation.5 | async-start | bytes 2621440 | tf_op jit(solution)/shard_map/psum | solution.py:11
  561.4 65.8 %copy-start.1 = (f32[2560,256]{0,1:T(8,128)S(1)}, f32[2560,256]{0,1:T(8,128)}, u32[]{:S(2)}) copy-start(f32[2560,256]{0,1:T(8,128)} %all-reduce.16.cloned.1.call-done) | copy-start | bytes 7864324
Sparse Core Ops, SparseCore 0:
  22.2 62.5 all-reduce.7
  154.3 91.5 all-reduce.9
  252.0 62.9 all-reduce.11
  338.1 59.2 all-reduce.13
  466.5 91.5 all-reduce.15
  564.3 62.9 all-reduce.17
where the time goes:
time: 679 us; the launch traced here: 669 us
  waiting for transfers between devices  429 us (63%)
  other arithmetic  131 us (19%)
  local copies, waits for them, and re-layouts  48.9 us (7%)
  matrix products  42.5 us (6%)
  between operations  16.8 us (2%)
    psum x6, waiting for transfers between devices, spread(): return lax.psum(block, axis)  429 us
    another operation x13, other arithmetic, solve_panel(): lower_factor = jnp.tril(jnp.linalg.cholesky(diagonal))  68.7 us
    another operation x5, other arithmetic, solve_panel(): jax.scipy.linalg.solve_triangular(lower_factor, column.T, lower=True)  39.4 us
    dot_general x2, matrix products, outer_update(): lax.dot_general(row_panel, col_panel, (((1,), (1,)), ((), ())), precision...  32.9 us
    unnamed x9, local copies, waits for them, and re-layouts  15.4 us
    scatter x1, local copies, waits for them, and re-layouts, finish(): return updated.at[:, :NB].set(first_cols)  13.9 us
  transfers between devices with their start and end apart: 6, of which 6 were waited for; matrix products, arithmetic and copies ran while one was open for 0% of the time, Pallas kernels for 0%

commit v1 on v0

v1 whole, which is shorter than its diff:
```python
import functools
import jax, jax.numpy as jnp
from jax import lax
from jax.experimental import pallas as pl
from jax.experimental.pallas import tpu as pltpu
P = jax.sharding.PartitionSpec
MESH = pl.DeviceIdType.MESH
HI = lax.Precision.HIGHEST
F32 = jnp.float32
BF16 = jnp.bfloat16
NB = 256
ROWS = 2560
COLS = 1280
CHUNK = 128
CHUNKS = ROWS // CHUNK
STRIP = 16
STRIPS = NB // STRIP
FIRST_STEP = 10
LAST_STEP = 17

def mm(a, b):
    return lax.dot_general(a, b, (((1,), (0,)), ((), ())), precision=HI, preferred_element_type=F32)

def mmt(a, b):
    return lax.dot_general(a, b, (((1,), (1,)), ((), ())), precision=HI, preferred_element_type=F32)

def full(v):
    return jnp.broadcast_to(v, (8, 128))

def leaf(w, start):
    lane = lax.broadcasted_iota(jnp.int32, (8, 128), 1)
    sub = lax.broadcasted_iota(jnp.int32, (8, 128), 0)
    other = (lane < 64) if start else (lane >= 64)
    rows = [w[8 * i:8 * i + 8, :] for i in range(8)]
    out = []
    for b in range(8):
        c = start + 8 * b
        bc = {i: [full(rows[i][:, c + k:c + k + 1]) for k in range(8)] for i in range(b, 8)}
        e = {(l, k): full(bc[b][k][l:l + 1, :]) for k in range(8) for l in range(k, 8)}
        u = [full(rows[b][k:k + 1, :]) for k in range(8)]
        done = jnp.zeros((8, 128), F32)
        for k in range(8):
            inv = 1.0 / e[k, k]
            for m in range(k + 1, 8):
                t = e[m, k] * inv
                for l in range(m, 8):
                    e[l, m] = e[l, m] - t * e[l, k]
                u[m] = u[m] - t * u[k]
                for i in range(b + 1, 8):
                    bc[i][m] = bc[i][m] - t * bc[i][k]
            scaled = u[k] * inv
            for i in range(b + 1, 8):
                rows[i] = rows[i] - bc[i][k] * scaled
            done = jnp.where(sub == k, u[k] * lax.rsqrt(e[k, k]), done)
        out.append(jnp.where(other, done, 0.0))
    return jnp.concatenate(out, axis=0)

def chol128(s):
    r = lax.broadcasted_iota(jnp.int32, (64, 128), 0)
    c = lax.broadcasted_iota(jnp.int32, (64, 128), 1)
    low = jnp.where(c == r, 1.0, 0.0)
    high = jnp.where(c == r + 64, 1.0, 0.0)
    first = leaf(jnp.where(c < 64, s[:64], high), 0)
    ma = pltpu.roll(first, 64, 1)
    l21 = mmt(jnp.where(c < 64, s[64:], 0.0), ma)
    s22 = mmt(l21, l21)
    z = jnp.zeros((64, 64), F32)
    s22 = jnp.concatenate([z, s22], axis=1)
    t = mm(l21, ma)
    second = leaf(jnp.where(c < 64, low, s[64:] - s22), 64)
    low_part = mm(second[:, :64], high - t)
    return jnp.concatenate([ma, low_part], axis=0)


PARENTS = (
    (
        (-1, 0, 3, 0, 8, 9, 10, 11, 12, 8, 14, 8, 0, 12, 15, 12),
        (1, -1, 14, 15, 5, 1, 5, 6, 9, 13, 9, 15, 13, 1, 13, 14),
    ),
    (
        (-1, 5, 6, 7, 0, 4, 7, 4, 4, 5, 11, 7, 8, 9, 10, 11),
        (3, -1, 1, 2, 7, 6, 2, 3, 11, 10, 6, 10, 15, 14, 2, 3),
    ),
)


def neighbour(chip, direction):
    y, x = chip // 4, chip % 4
    if direction < 2:
        return y * 4 + (x + (1, 3)[direction]) % 4
    return (y + (1, 3)[direction - 2]) % 4 * 4 + x


def senders(core, panel, direction):
    parents = PARENTS[core][panel]
    return [n for n in range(16) if parents[neighbour(n, direction)] == n]


MESSAGES = (
    (0, 0, 0, 0),
    (0, 1, 0, 1),
    (0, 1, 1, 2),
    (1, 0, 0, 0),
    (1, 0, 1, 1),
    (1, 1, 0, 2),
    (1, 1, 1, 0),
    (2, 0, 0, 0),
    (2, 1, 0, 1),
    (2, 1, 1, 2),
)


def panels_kernel(
    a_ref, r_ref, ct_ref, rows, slab, fac, diag, stage, lead, inv, low,
    local_sem, row_send, row_recv, slab_send, slab_recv, fac_send, fac_recv, diag_sem,
):
    prow, pcol = lax.axis_index("prow"), lax.axis_index("pcol")
    z, core = prow // 2, prow % 2
    y, x = pcol // 4, pcol % 4
    is_root = jnp.logical_and(prow == 0, pcol == 0)
    gives_diag = jnp.logical_and(prow == 1, pcol == 1)

    def device(pz, pc, py, px):
        return {"prow": pz * 2 + pc, "pcol": py * 4 + px}

    def on_line(axis, step):
        if axis == "x":
            return device(z, core, y, (x + step) % 4)
        if axis == "y":
            return device(z, core, (y + step) % 4, x)
        return device((z + step) % 4, core, y, x)

    sibling = device(z, 1 - core, y, x)

    barrier = pltpu.get_barrier_semaphore()
    for axis in "xyz":
        for step in (1, 2, 3):
            pl.semaphore_signal(barrier, 1, device_id=on_line(axis, step), device_id_type=MESH)
    pl.semaphore_signal(barrier, 1, device_id=sibling, device_id_type=MESH)

    @pl.when(is_root)
    def _():
        pl.semaphore_signal(barrier, 1, device_id={"prow": 1, "pcol": 1}, device_id_type=MESH)

    pl.semaphore_wait(barrier, 10 + jnp.where(gives_diag, 1, 0))

    index = core * 16 + pcol
    gives = [[None] * 4 for _ in range(2)]
    for k in range(2):
        for d in range(4):
            flag = jnp.int32(0)
            for c in range(2):
                for n in senders(c, k, d):
                    flag = flag + jnp.where(index == c * 16 + n, 1, 0)
            gives[k][d] = flag == 1
    targets = (on_line("x", 1), on_line("x", 3), on_line("y", 1), on_line("y", 3))

    def row_copy(src, k, d, first, count):
        piece = pl.ds(first, count)
        return pltpu.make_async_remote_copy(
            src_ref=src.at[piece, pl.ds(0, NB)] if src is a_ref else rows.at[k, piece, :],
            dst_ref=rows.at[k, piece, :],
            send_sem=row_send.at[k, d],
            recv_sem=row_recv.at[k, first // CHUNK if count == CHUNK else 0],
            device_id=targets[d],
            device_id_type=MESH,
        )

    def slab_copy(src, s, slot, first, count):
        piece = pl.ds(first, count)
        step = 1 if s == 0 else 3
        return pltpu.make_async_remote_copy(
            src_ref=a_ref.at[piece, :] if src is a_ref else slab.at[s, piece, :],
            dst_ref=slab.at[s, piece, :],
            send_sem=slab_send.at[s, slot],
            recv_sem=slab_recv.at[s, first // STRIP if count == STRIP else 0],
            device_id=on_line("z", step) if slot == 0 else sibling,
            device_id_type=MESH,
        )

    along = (
        jnp.logical_and(core == 0, z < 3),
        jnp.logical_and(core == 1, z != 1),
    )
    across = (core == 0, core == 1)

    def own_rows(k):
        return pltpu.make_async_copy(a_ref.at[:, pl.ds(0, NB)], rows.at[k], local_sem.at[k])

    def own_slab(s):
        return pltpu.make_async_copy(a_ref.at[pl.ds(0, NB), :], slab.at[s], local_sem.at[2 + s])

    def diag_copy():
        return pltpu.make_async_remote_copy(
            src_ref=a_ref.at[pl.ds(0, NB), pl.ds(0, NB)],
            dst_ref=diag,
            send_sem=diag_sem.at[0],
            recv_sem=diag_sem.at[1],
            device_id={"prow": 0, "pcol": 0},
            device_id_type=MESH,
        )

    @pl.when(gives_diag)
    def _():
        diag_copy().start()

    for s in range(2):
        @pl.when(prow == s)
        def _(s=s):
            own_slab(s).start()

    for k in range(2):
        @pl.when(pcol == k)
        def _(k=k):
            own_rows(k).start()

            def send(i, carry):
                for d in range(4):
                    @pl.when(gives[k][d])
                    def _(d=d):
                        row_copy(a_ref, k, d, i * CHUNK, CHUNK).start()
                return carry

            lax.fori_loop(0, CHUNKS, send, 0)

    for s in range(2):
        @pl.when(prow == s)
        def _(s=s):
            def send(j, carry):
                slab_copy(a_ref, s, 0, j * STRIP, STRIP).start()
                slab_copy(a_ref, s, 1, j * STRIP, STRIP).start()
                return carry

            lax.fori_loop(0, STRIPS, send, 0)

    def pass_rows(i):
        for k in range(2):
            @pl.when(pcol != k)
            def _(k=k):
                row_copy(None, k, 0, i * CHUNK, CHUNK).wait_recv()
                for d in range(4):
                    @pl.when(gives[k][d])
                    def _(d=d):
                        row_copy(None, k, d, i * CHUNK, CHUNK).start()

    def pass_slab(j):
        for s in range(2):
            @pl.when(jnp.logical_and(prow != s, jnp.logical_not(is_root)))
            def _(s=s):
                slab_copy(None, s, 0, j * STRIP, STRIP).wait_recv()

                @pl.when(along[s])
                def _():
                    slab_copy(None, s, 0, j * STRIP, STRIP).start()

                @pl.when(across[s])
                def _():
                    slab_copy(None, s, 1, j * STRIP, STRIP).start()

    where = {"x": x, "y": y, "z": z}

    def fac_targets(q):
        order = ("xyz", "yzx", "zxy")[MESSAGES[q][3]]
        at = [where[a] == 0 for a in order]
        first = jnp.logical_and(core == 0, jnp.logical_and(at[1], at[2]))
        conditions = (
            jnp.logical_and(first, at[0]),
            first,
            jnp.logical_and(core == 0, at[2]),
        )
        found = []
        for stage_index, axis in enumerate(order):
            for step in (2, 1, 3):
                found.append((conditions[stage_index], on_line(axis, step)))
        found.append((core == 0, sibling))
        return found

    def fac_copy(q, slot, target):
        m, i, j, _ = MESSAGES[q]
        piece = fac.at[m, pl.ds(i * 128, 128), pl.ds(j * 128, 128)]
        return pltpu.make_async_remote_copy(
            src_ref=piece,
            dst_ref=piece,
            send_sem=fac_send.at[q, slot],
            recv_sem=fac_recv.at[q],
            device_id=target,
            device_id_type=MESH,
        )

    def fac_start(q):
        for slot, (condition, target) in enumerate(fac_targets(q)):
            @pl.when(condition)
            def _(slot=slot, target=target):
                fac_copy(q, slot, target).start()

    def fac_pass(queue):
        @pl.when(jnp.logical_not(is_root))
        def _():
            for q in queue:
                fac_copy(q, 0, sibling).wait_recv()
                fac_start(q)

    for m in (0, 2):
        fac[m, 0:128, 128:256] = jnp.zeros((128, 128), F32)

    @pl.when(is_root)
    def _():
        own_slab(0).wait()
        stage[...] = slab[0, :, 0:NB]

        def panel(k, carry):
            lead[...] = stage[0:128, 0:128]

            def half(h, inner):
                inv[h] = chol128(lead[...])

                @pl.when(h == 0)
                def _():
                    low[...] = mmt(stage[128:256, 0:128], inv[0])
                    lead[...] = stage[128:256, 128:256] - mmt(low[...], low[...])

                return inner

            lax.fori_loop(0, 2, half, 0)
            fac[2 * k, 0:128, 0:128] = inv[0]
            fac[2 * k, 128:256, 128:256] = inv[1]
            fac[2 * k, 128:256, 0:128] = -mm(inv[1], mm(low[...], inv[0]))

            @pl.when(k == 0)
            def _():
                for q in (0, 1, 2):
                    fac_start(q)

                def arrive(j, inner):
                    slab_copy(None, 1, 0, j * STRIP, STRIP).wait_recv()
                    return inner

                lax.fori_loop(0, STRIPS, arrive, 0)
                below = mmt(slab[1, :, 0:NB], fac[0])
                fac[1] = below
                for q in (3, 4, 5, 6):
                    fac_start(q)
                diag_copy().wait_recv()
                stage[...] = diag[...] - mmt(below, below)

            @pl.when(k == 1)
            def _():
                for q in (7, 8, 9):
                    fac_start(q)

            return carry

        lax.fori_loop(0, 2, panel, 0)

    for k in range(2):
        @pl.when(pcol == k)
        def _(k=k):
            own_rows(k).wait()

    @pl.when(jnp.logical_and(prow == 0, jnp.logical_not(is_root)))
    def _():
        own_slab(0).wait()

    @pl.when(prow == 1)
    def _():
        own_slab(1).wait()

    def early(i, carry):
        pass_rows(i)
        pass_slab(i)
        return carry

    def late(i, carry):
        pass_rows(i)

        @pl.when(i < STRIPS)
        def _():
            pass_slab(i)

        block = pl.ds(pl.multiple_of((i - FIRST_STEP) * NB, NB), NB)
        first = mmt(rows[0, block, :], fac[0])
        r_ref[block, 0:NB] = first
        r_ref[block, NB:2 * NB] = rows[1, block, :] - mmt(first, fac[1])
        return carry

    lax.fori_loop(0, FIRST_STEP, early, 0)
    fac_pass((0, 1, 2, 3, 4, 5, 6))
    lax.fori_loop(FIRST_STEP, LAST_STEP, late, 0)
    fac_pass((7, 8, 9))
    lax.fori_loop(LAST_STEP, CHUNKS, late, 0)

    def columns(j, carry):
        tile = pl.ds(pl.multiple_of(j * NB, NB), NB)
        first = mm(fac[0], slab[0, :, tile])
        ct_ref[0:NB, tile] = first
        ct_ref[NB:2 * NB, tile] = mm(fac[2], slab[1, :, tile] - mm(fac[1], first))
        return carry

    lax.fori_loop(0, COLS // NB, columns, 0)

    def second(j, carry):
        block = pl.ds(pl.multiple_of(j * NB, NB), NB)
        r_ref[block, NB:2 * NB] = mmt(r_ref[block, NB:2 * NB], fac[2])
        return carry

    lax.fori_loop(0, ROWS // NB, second, 0)

    for k in range(2):
        for d in range(4):
            @pl.when(gives[k][d])
            def _(k=k, d=d):
                row_copy(None, k, d, 0, ROWS).wait_send()

    for s in range(2):
        for slot, condition in enumerate((along[s], across[s])):
            @pl.when(condition)
            def _(s=s, slot=slot):
                slab_copy(None, s, slot, 0, NB).wait_send()

    for q in range(len(MESSAGES)):
        for slot, (condition, target) in enumerate(fac_targets(q)):
            @pl.when(condition)
            def _(q=q, slot=slot, target=target):
                fac_copy(q, slot, target).wait_send()

    @pl.when(gives_diag)
    def _():
        diag_copy().wait_send()


def make_panels(matrix):
    dma = pltpu.SemaphoreType.DMA
    vmem = pl.BlockSpec(memory_space=pltpu.VMEM)
    return pl.pallas_call(
        panels_kernel,
        out_shape=(
            jax.ShapeDtypeStruct((ROWS, 2 * NB), F32),
            jax.ShapeDtypeStruct((2 * NB, COLS), F32),
        ),
        in_specs=[pl.BlockSpec(memory_space=pl.ANY)],
        out_specs=(vmem, vmem),
        scratch_shapes=[
            pltpu.VMEM((2, ROWS, NB), F32),
            pltpu.VMEM((2, NB, COLS), F32),
            pltpu.VMEM((3, NB, NB), F32),
            pltpu.VMEM((NB, NB), F32),
            pltpu.VMEM((NB, NB), F32),
            pltpu.VMEM((128, 128), F32),
            pltpu.VMEM((2, 128, 128), F32),
            pltpu.VMEM((128, 128), F32),
            dma((4,)),
            dma((2, 4)),
            dma((2, CHUNKS)),
            dma((2, 2)),
            dma((2, STRIPS)),
            dma((len(MESSAGES), 10)),
            dma((len(MESSAGES),)),
            dma((2,)),
        ],
        compiler_params=pltpu.CompilerParams(
            collective_id=0, has_side_effects=True, vmem_limit_bytes=40 * 2**20
        ),
        cost_estimate=pl.CostEstimate(
            flops=2 * 3 * ROWS * NB * NB, bytes_accessed=2**24, transcendentals=0
        ),
        name="panels",
    )(matrix)


def update_kernel(place, a_ref, r_ref, ct_ref, out_ref, c_high, c_low):
    i = pl.program_id(0)

    @pl.when(i == 0)
    def _():
        def split(j, carry):
            strip = pl.ds(pl.multiple_of(j * 64, 64), 64)
            value = ct_ref[strip, :]
            high = value.astype(BF16)
            c_high[strip, :] = high
            c_low[strip, :] = (value - high.astype(F32)).astype(BF16)
            return carry

        lax.fori_loop(0, 2 * NB // 64, split, 0)

    prow, pcol = place[0], place[1]
    row_block = i * 8 + prow
    value = r_ref[...]
    high = value.astype(BF16)
    low = (value - high.astype(F32)).astype(BF16)

    def dot(a, b):
        return lax.dot_general(a, b, (((1,), (0,)), ((), ())), preferred_element_type=F32)

    def update(j):
        tile = pl.ds(j * NB, NB)
        product = dot(high, c_high[:, tile]) + dot(high, c_low[:, tile]) + dot(low, c_high[:, tile])
        out_ref[:, tile] = a_ref[:, tile] - product

    for j in range(COLS // NB):
        tile = pl.ds(j * NB, NB)
        stays = row_block >= 2
        if j == 0:
            stays = jnp.logical_and(stays, pcol >= 2)

        @pl.when(stays)
        def _(j=j):
            update(j)

        @pl.when(jnp.logical_not(stays))
        def _(tile=tile):
            out_ref[:, tile] = jnp.zeros((NB, NB), F32)

    down = lax.broadcasted_iota(jnp.int32, (NB, NB), 0)
    right = lax.broadcasted_iota(jnp.int32, (NB, NB), 1)
    for k in range(2):
        @pl.when(jnp.logical_and(pcol == k, row_block >= k))
        def _(k=k):
            keep = jnp.logical_or(row_block > k, right <= down)
            out_ref[:, 0:NB] = jnp.where(keep, r_ref[:, k * NB:(k + 1) * NB], 0.0)


def update(matrix, row_panel, col_panel):
    place = jnp.stack([lax.axis_index("prow"), lax.axis_index("pcol")]).astype(jnp.int32)
    return pl.pallas_call(
        update_kernel,
        out_shape=jax.ShapeDtypeStruct((ROWS, COLS), F32),
        grid=(ROWS // NB,),
        in_specs=[
            pl.BlockSpec(memory_space=pltpu.SMEM),
            pl.BlockSpec((NB, COLS), lambda i: (i, 0)),
            pl.BlockSpec((NB, 2 * NB), lambda i: (i, 0)),
            pl.BlockSpec((2 * NB, COLS), lambda i: (0, 0)),
        ],
        out_specs=pl.BlockSpec((NB, COLS), lambda i: (i, 0)),
        scratch_shapes=[pltpu.VMEM((2 * NB, COLS), BF16), pltpu.VMEM((2 * NB, COLS), BF16)],
        compiler_params=pltpu.CompilerParams(vmem_limit_bytes=40 * 2**20),
        cost_estimate=pl.CostEstimate(
            flops=2 * 3 * ROWS * COLS * 2 * NB, bytes_accessed=2**25, transcendentals=0
        ),
        name="update",
    )(place, matrix, row_panel, col_panel)


def body(matrix):
    row_panel, col_panel = make_panels(matrix)
    return update(matrix, row_panel, col_panel)


def solution(mesh):
    spec = P("prow", "pcol")
    return jax.shard_map(body, mesh=mesh, in_specs=(spec,), out_specs=spec, check_vma=False)
```

time: 679 us -> 557 us (0.82)
  the two profiles are of different devices: /device:TPU:0 before, /device:TPU:45 now
where the time goes in v1:
time: 557 us; the launch traced here: 546 us
  Pallas kernels  546 us (98%)
    pallas_call x1, Pallas kernels, make_panels(): pl.pallas_call(panels_kernel, out_shape=(jax.ShapeDtypeStruct((ROWS, 2 *...  523 us
    pallas_call x1, Pallas kernels, update(): pl.pallas_call(update_kernel, out_shape=jax.ShapeDtypeStruct((ROWS, COLS)...  23 us

profile of v1, /device:TPU:45, one launch (start us, length us, event | category | flops | bytes accessed | tf_op | source)
XLA Modules:
  0.0 546.2 jit_solution(17933993203634650441)
XLA Ops:
  0.0 0.1 pad_add_fusion.place
  0.1 523.1 %panels.1 = (f32[2560,512]{1,0:T(8,128)S(1)}, f32[512,1280]{1,0:T(8,128)S(1)}) custom-call(f32[2560,1280]{1,0:T(8,128)} %a_ref.3), custom_call_target="tpu_custom_call" | custom-call | flops 1006632960 | bytes 16777216 | tf_op jit(solution)/shard_map/panels/pallas_call | solution.py:434
  523.2 23.0 %update.1 = f32[2560,1280]{1,0:T(8,128)} custom-call(s32[2]{0:T(128)S(1)} %pad_add_fusion.place, f32[2560,1280]{1,0:T(8,128)} %a_ref.3, f32[2560,512]{1,0:T(8,128)S(1)} %get-tuple-element.7.r_ref, f32[512,1280]{1,0:T(8,128)S(1)} %get-tuple-element.8.ct_ref), custom_call_target="tpu_custom_call" | custom-call | flops 10066329600 | bytes 33554432 | tf_op jit(solution)/shard_map/update/pallas_call | solution.py:524

commit v2 on v1

--- a/solution.py
+++ b/solution.py
@@ -11,18 +11,36 @@
 NB = 256
 ROWS = 2560
 COLS = 1280
-CHUNK = 128
+CHUNK = 64
 CHUNKS = ROWS // CHUNK
 STRIP = 16
 STRIPS = NB // STRIP
-FIRST_STEP = 10
-LAST_STEP = 17
+LAG = 4
+DEEPEST = 5
+TICKS = CHUNKS + LAG * DEEPEST
+FIRST_FACTOR = 18
+SECOND_FACTOR = 34
+COLUMNS_TICK = 35
+BLOCKS_TICK = TICKS - 2 * (ROWS // NB) + 1
 
 def mm(a, b):
     return lax.dot_general(a, b, (((1,), (0,)), ((), ())), precision=HI, preferred_element_type=F32)
 
 def mmt(a, b):
     return lax.dot_general(a, b, (((1,), (1,)), ((), ())), precision=HI, preferred_element_type=F32)
+
+def split(v):
+    high = v.astype(BF16)
+    return high, (v - high.astype(F32)).astype(BF16)
+
+
+def three(a, b_high, b_low):
+    def dot(p, q):
+        return lax.dot_general(p, q, (((1,), (0,)), ((), ())), preferred_element_type=F32)
+
+    high, low = split(a)
+    return dot(high, b_high) + dot(high, b_low) + dot(low, b_high)
+
 
 def full(v):
     return jnp.broadcast_to(v, (8, 128))
@@ -91,6 +109,11 @@
     return (y + (1, 3)[direction - 2]) % 4 * 4 + x
 
 
+def depth(core, panel, chip):
+    parent = PARENTS[core][panel][chip]
+    return 0 if parent < 0 else 1 + depth(core, panel, parent)
+
+
 def senders(core, panel, direction):
     parents = PARENTS[core][panel]
     return [n for n in range(16) if parents[neighbour(n, direction)] == n]
@@ -111,7 +134,7 @@
 
 
 def panels_kernel(
-    a_ref, r_ref, ct_ref, rows, slab, fac, diag, stage, lead, inv, low,
+    a_ref, w_ref, r_ref, ct_ref, rows, slab, first_ct, fac, diag, stage, lead, inv, low,
     local_sem, row_send, row_recv, slab_send, slab_recv, fac_send, fac_recv, diag_sem,
 ):
     prow, pcol = lax.axis_index("prow"), lax.axis_index("pcol")
@@ -153,6 +176,17 @@
                 for n in senders(c, k, d):
                     flag = flag + jnp.where(index == c * 16 + n, 1, 0)
             gives[k][d] = flag == 1
+    depths = []
+    for k in range(2):
+        value = jnp.int32(0)
+        for c in range(2):
+            for n in range(16):
+                value = value + jnp.where(index == c * 16 + n, depth(c, k, n), 0)
+        depths.append(value)
+    slab_depths = (z + core, (4 - z) % 4 + 1 - core)
+    fac_depth = core
+    for coordinate in (x, y, z):
+        fac_depth = fac_depth + jnp.where(coordinate != 0, 1, 0)
     targets = (on_line("x", 1), on_line("x", 3), on_line("y", 1), on_line("y", 3))
 
     def row_copy(src, k, d, first, count):
@@ -200,6 +234,11 @@
             device_id_type=MESH,
         )
 
+    def own_block():
+        return pltpu.make_async_copy(a_ref, w_ref, local_sem.at[4])
+
+    own_block().start()
+
     @pl.when(gives_diag)
     def _():
         diag_copy().start()
@@ -233,20 +272,27 @@
 
             lax.fori_loop(0, STRIPS, send, 0)
 
-    def pass_rows(i):
+    def pass_rows(tick):
         for k in range(2):
-            @pl.when(pcol != k)
-            def _(k=k):
+            i = tick - LAG * depths[k]
+            here = jnp.logical_and(i >= 0, i < CHUNKS)
+
+            @pl.when(jnp.logical_and(here, pcol != k))
+            def _(k=k, i=i):
                 row_copy(None, k, 0, i * CHUNK, CHUNK).wait_recv()
                 for d in range(4):
                     @pl.when(gives[k][d])
                     def _(d=d):
                         row_copy(None, k, d, i * CHUNK, CHUNK).start()
 
-    def pass_slab(j):
+    def pass_slab(tick):
         for s in range(2):
-            @pl.when(jnp.logical_and(prow != s, jnp.logical_not(is_root)))
-            def _(s=s):
+            j = tick - LAG * slab_depths[s]
+            here = jnp.logical_and(j >= 0, j < STRIPS)
+            here = jnp.logical_and(here, jnp.logical_not(is_root))
+
+            @pl.when(jnp.logical_and(here, prow != s))
+            def _(s=s, j=j):
                 slab_copy(None, s, 0, j * STRIP, STRIP).wait_recv()
 
                 @pl.when(along[s])
@@ -365,42 +411,58 @@
     def _():
         own_slab(1).wait()
 
-    def early(i, carry):
-        pass_rows(i)
-        pass_slab(i)
+    own_block().wait()
+
+    def step(tick, carry):
+        pass_rows(tick)
+        pass_slab(tick)
+
+        @pl.when(tick == FIRST_FACTOR + LAG * fac_depth)
+        def _():
+            fac_pass((0, 1, 2, 3, 4, 5, 6))
+
+        @pl.when(tick == SECOND_FACTOR + LAG * fac_depth)
+        def _():
+            fac_pass((7, 8, 9))
+
+        @pl.when(jnp.logical_and(tick >= COLUMNS_TICK, tick < COLUMNS_TICK + COLS // NB))
+        def _():
+            tile = pl.ds(pl.multiple_of((tick - COLUMNS_TICK) * NB, NB), NB)
+            first = mm(fac[0], slab[0, :, tile])
+            high, low_part = split(first)
+            first_ct[0, :, tile] = high
+            first_ct[1, :, tile] = low_part
+            ct_ref[:, tile] = slab[1, :, tile] - mm(fac[1], first)
+
+        @pl.when(jnp.logical_and(tick >= BLOCKS_TICK, (tick - BLOCKS_TICK) % 2 == 0))
+        def _():
+            i = (tick - BLOCKS_TICK) // 2
+            block = pl.ds(pl.multiple_of(i * NB, NB), NB)
+            first = mmt(rows[0, block, :], fac[0])
+            r_ref[block, :] = rows[1, block, :] - mmt(first, fac[1])
+            w_ref[block, :] = w_ref[block, :] - three(first, first_ct[0], first_ct[1])
+
+            @pl.when(pcol == 0)
+            def _():
+                down = lax.broadcasted_iota(jnp.int32, (NB, NB), 0)
+                right = lax.broadcasted_iota(jnp.int32, (NB, NB), 1)
+                keep = jnp.logical_or(i * 8 + prow > 0, right <= down)
+                w_ref[block, 0:NB] = jnp.where(keep, first, 0.0)
+
         return carry
 
-    def late(i, carry):
-        pass_rows(i)
-
-        @pl.when(i < STRIPS)
-        def _():
-            pass_slab(i)
-
-        block = pl.ds(pl.multiple_of((i - FIRST_STEP) * NB, NB), NB)
-        first = mmt(rows[0, block, :], fac[0])
-        r_ref[block, 0:NB] = first
-        r_ref[block, NB:2 * NB] = rows[1, block, :] - mmt(first, fac[1])
-        return carry
-
-    lax.fori_loop(0, FIRST_STEP, early, 0)
-    fac_pass((0, 1, 2, 3, 4, 5, 6))
-    lax.fori_loop(FIRST_STEP, LAST_STEP, late, 0)
-    fac_pass((7, 8, 9))
-    lax.fori_loop(LAST_STEP, CHUNKS, late, 0)
+    lax.fori_loop(0, TICKS, step, 0)
 
     def columns(j, carry):
         tile = pl.ds(pl.multiple_of(j * NB, NB), NB)
-        first = mm(fac[0], slab[0, :, tile])
-        ct_ref[0:NB, tile] = first
-        ct_ref[NB:2 * NB, tile] = mm(fac[2], slab[1, :, tile] - mm(fac[1], first))
+        ct_ref[:, tile] = mm(fac[2], ct_ref[:, tile])
         return carry
 
     lax.fori_loop(0, COLS // NB, columns, 0)
 
     def second(j, carry):
         block = pl.ds(pl.multiple_of(j * NB, NB), NB)
-        r_ref[block, NB:2 * NB] = mmt(r_ref[block, NB:2 * NB], fac[2])
+        r_ref[block, :] = mmt(r_ref[block, :], fac[2])
         return carry
 
     lax.fori_loop(0, ROWS // NB, second, 0)
@@ -434,21 +496,23 @@
     return pl.pallas_call(
         panels_kernel,
         out_shape=(
-            jax.ShapeDtypeStruct((ROWS, 2 * NB), F32),
-            jax.ShapeDtypeStruct((2 * NB, COLS), F32),
+            jax.ShapeDtypeStruct((ROWS, COLS), F32),
+            jax.ShapeDtypeStruct((ROWS, NB), F32),
+            jax.ShapeDtypeStruct((NB, COLS), F32),
         ),
         in_specs=[pl.BlockSpec(memory_space=pl.ANY)],
-        out_specs=(vmem, vmem),
+        out_specs=(vmem, vmem, vmem),
         scratch_shapes=[
             pltpu.VMEM((2, ROWS, NB), F32),
             pltpu.VMEM((2, NB, COLS), F32),
+            pltpu.VMEM((2, NB, COLS), BF16),
             pltpu.VMEM((3, NB, NB), F32),
             pltpu.VMEM((NB, NB), F32),
             pltpu.VMEM((NB, NB), F32),
             pltpu.VMEM((128, 128), F32),
             pltpu.VMEM((2, 128, 128), F32),
             pltpu.VMEM((128, 128), F32),
-            dma((4,)),
+            dma((5,)),
             dma((2, 4)),
             dma((2, CHUNKS)),
             dma((2, 2)),
@@ -458,92 +522,73 @@
             dma((2,)),
         ],
         compiler_params=pltpu.CompilerParams(
-            collective_id=0, has_side_effects=True, vmem_limit_bytes=40 * 2**20
+            collective_id=0, has_side_effects=True, vmem_limit_bytes=36 * 2**20
         ),
         cost_estimate=pl.CostEstimate(
-            flops=2 * 3 * ROWS * NB * NB, bytes_accessed=2**24, transcendentals=0
+            flops=2 * 3 * ROWS * NB * COLS, bytes_accessed=2**24, transcendentals=0
         ),
         name="panels",
     )(matrix)
 
 
-def update_kernel(place, a_ref, r_ref, ct_ref, out_ref, c_high, c_low):
+def update_kernel(place, w_ref, r_ref, ct_ref, out_ref, c_high, c_low):
     i = pl.program_id(0)
 
     @pl.when(i == 0)
     def _():
-        def split(j, carry):
+        def cut(j, carry):
             strip = pl.ds(pl.multiple_of(j * 64, 64), 64)
-            value = ct_ref[strip, :]
-            high = value.astype(BF16)
-            c_high[strip, :] = high
-            c_low[strip, :] = (value - high.astype(F32)).astype(BF16)
+            c_high[strip, :], c_low[strip, :] = split(ct_ref[strip, :])
             return carry
 
-        lax.fori_loop(0, 2 * NB // 64, split, 0)
+        lax.fori_loop(0, NB // 64, cut, 0)
 
     prow, pcol = place[0], place[1]
     row_block = i * 8 + prow
-    value = r_ref[...]
-    high = value.astype(BF16)
-    low = (value - high.astype(F32)).astype(BF16)
-
-    def dot(a, b):
-        return lax.dot_general(a, b, (((1,), (0,)), ((), ())), preferred_element_type=F32)
-
-    def update(j):
-        tile = pl.ds(j * NB, NB)
-        product = dot(high, c_high[:, tile]) + dot(high, c_low[:, tile]) + dot(low, c_high[:, tile])
-        out_ref[:, tile] = a_ref[:, tile] - product
-
-    for j in range(COLS // NB):
-        tile = pl.ds(j * NB, NB)
-        stays = row_block >= 2
-        if j == 0:
-            stays = jnp.logical_and(stays, pcol >= 2)
-
-        @pl.when(stays)
-        def _(j=j):
-            update(j)
-
-        @pl.when(jnp.logical_not(stays))
-        def _(tile=tile):
-            out_ref[:, tile] = jnp.zeros((NB, NB), F32)
-
-    down = lax.broadcasted_iota(jnp.int32, (NB, NB), 0)
-    right = lax.broadcasted_iota(jnp.int32, (NB, NB), 1)
-    for k in range(2):
-        @pl.when(jnp.logical_and(pcol == k, row_block >= k))
-        def _(k=k):
-            keep = jnp.logical_or(row_block > k, right <= down)
-            out_ref[:, 0:NB] = jnp.where(keep, r_ref[:, k * NB:(k + 1) * NB], 0.0)
-
-
-def update(matrix, row_panel, col_panel):
+    block = pl.ds(pl.multiple_of(i * NB, NB), NB)
+    out_ref[...] = w_ref[block, :] - three(r_ref[block, :], c_high[...], c_low[...])
+
+    @pl.when(row_block < 2)
+    def _():
+        out_ref[:, NB:COLS] = jnp.zeros((NB, COLS - NB), F32)
+
+        @pl.when(pcol > row_block)
+        def _():
+            out_ref[:, 0:NB] = jnp.zeros((NB, NB), F32)
+
+    @pl.when(pcol == 0)
+    def _():
+        out_ref[:, 0:NB] = w_ref[block, 0:NB]
+
+    @pl.when(jnp.logical_and(pcol == 1, row_block >= 1))
+    def _():
+        down = lax.broadcasted_iota(jnp.int32, (NB, NB), 0)
+        right = lax.broadcasted_iota(jnp.int32, (NB, NB), 1)
+        keep = jnp.logical_or(row_block > 1, right <= down)
+        out_ref[:, 0:NB] = jnp.where(keep, r_ref[block, :], 0.0)
+
+
+def update(first_update, row_panel, col_panel):
     place = jnp.stack([lax.axis_index("prow"), lax.axis_index("pcol")]).astype(jnp.int32)
+    vmem = pl.BlockSpec(memory_space=pltpu.VMEM)
     return pl.pallas_call(
         update_kernel,
         out_shape=jax.ShapeDtypeStruct((ROWS, COLS), F32),
         grid=(ROWS // NB,),
-        in_specs=[
-            pl.BlockSpec(memory_space=pltpu.SMEM),
-            pl.BlockSpec((NB, COLS), lambda i: (i, 0)),
-            pl.BlockSpec((NB, 2 * NB), lambda i: (i, 0)),
-            pl.BlockSpec((2 * NB, COLS), lambda i: (0, 0)),
-        ],
+        in_specs=[pl.BlockSpec(memory_space=pltpu.SMEM), vmem, vmem, vmem],
         out_specs=pl.BlockSpec((NB, COLS), lambda i: (i, 0)),
-        scratch_shapes=[pltpu.VMEM((2 * NB, COLS), BF16), pltpu.VMEM((2 * NB, COLS), BF16)],
-        compiler_params=pltpu.CompilerParams(vmem_limit_bytes=40 * 2**20),
+        scratch_shapes=[pltpu.VMEM((NB, COLS), BF16), pltpu.VMEM((NB, COLS), BF16)],
+        compiler_params=pltpu.CompilerParams(vmem_limit_bytes=36 * 2**20),
         cost_estimate=pl.CostEstimate(
-            flops=2 * 3 * ROWS * COLS * 2 * NB, bytes_accessed=2**25, transcendentals=0
+            flops=2 * 3 * ROWS * COLS * NB, bytes_accessed=2**24, transcendentals=0
         ),
         name="update",
-    )(place, matrix, row_panel, col_panel)
+    )(place, first_update, row_panel, col_panel)
 
 
 def body(matrix):
-    row_panel, col_panel = make_panels(matrix)
-    return update(matrix, row_panel, col_panel)
+    first_update, row_panel, col_panel = make_panels(matrix)
+    return update(first_update, row_panel, col_panel)
 
 
 def solution(mesh):

time: 557 us -> 100 us (0.18)
  the two profiles are of different devices: /device:TPU:45 before, /device:TPU:14 now
where the time goes in v2:
time: 100 us
  Pallas kernels  100 us (100%)
    pallas_call x1, Pallas kernels, make_panels(): pl.pallas_call(panels_kernel, out_shape=(jax.ShapeDtypeStruct((ROWS, COLS...  89.8 us
    pallas_call x1, Pallas kernels, update(): pl.pallas_call(update_kernel, out_shape=jax.ShapeDtypeStruct((ROWS, COLS)...  10.4 us

profile of v2, /device:TPU:14, one launch (start us, length us, event | category | flops | bytes accessed | tf_op | source)
XLA Modules:
  0.0 100.3 jit_solution(17963109168968864711)
XLA Ops:
  0.0 0.1 pad_add_fusion.place
  0.1 89.8 %panels.1 = (f32[2560,1280]{1,0:T(8,128)S(1)}, f32[2560,256]{1,0:T(8,128)S(1)}, f32[256,1280]{1,0:T(8,128)S(1)}) custom-call(f32[2560,1280]{1,0:T(8,128)} %a_ref.1), custom_call_target="tpu_custom_call" | custom-call | flops 5033164800 | bytes 16777216 | tf_op jit(solution)/shard_map/panels/pallas_call | solution.py:496
  89.9 10.4 %update.1 = f32[2560,1280]{1,0:T(8,128)} custom-call(s32[2]{0:T(128)S(1)} %pad_add_fusion.place, f32[2560,1280]{1,0:T(8,128)S(1)} %get-tuple-element.8.w_ref, f32[2560,256]{1,0:T(8,128)S(1)} %get-tuple-element.9.r_ref, f32[256,1280]{1,0:T(8,128)S(1)} %get-tuple-element.10.ct_ref), custom_call_target="tpu_custom_call" | custom-call | flops 5033164800 | bytes 16777216 | tf_op jit(solution)/shard_map/update/pallas_call | solution.py:574

commit v3 on v2

v3 whole, which is shorter than its diff:
```python
import jax
import jax.numpy as jnp
from jax import lax
from jax.experimental import pallas as pl
from jax.experimental.pallas import tpu as pltpu

P = jax.sharding.PartitionSpec
MESH = pl.DeviceIdType.MESH
HI = lax.Precision.HIGHEST
F32 = jnp.float32
BF16 = jnp.bfloat16
NB = 256
HALF = NB // 2
ROWS = 2560
COLS = 1280
CHUNK = 64
CHUNKS = ROWS // CHUNK
STRIP = 16
STRIPS = NB // STRIP
BLOCKS = (3, 4, 3)
FIRST_MESSAGE = (0, 3, 7)
PLACES = (25, 29, 42)
ITEMS = CHUNKS + len(PLACES)
LAG = 4
DEEPEST = 5
TICKS = ITEMS + LAG * DEEPEST
SLAB_TICK = 12
AHEAD = 6
PUMP = 5


def mm(a, b):
    return lax.dot_general(a, b, (((1,), (0,)), ((), ())), precision=HI, preferred_element_type=F32)


def mmt(a, b):
    return lax.dot_general(a, b, (((1,), (1,)), ((), ())), precision=HI, preferred_element_type=F32)


def split(v):
    high = v.astype(BF16)
    return high, (v - high.astype(F32)).astype(BF16)


def three(a_high, a_low, b_high, b_low, contract=0):
    def dot(p, q):
        return lax.dot_general(p, q, (((1,), (contract,)), ((), ())), preferred_element_type=F32)

    return dot(a_high, b_high) + dot(a_high, b_low) + dot(a_low, b_high)


def three_t(a_high, a_low, b_high, b_low):
    return three(a_high, a_low, b_high, b_low, 1)


def full(v):
    return jnp.broadcast_to(v, (8, 128))

def leaf(w, start):
    lane = lax.broadcasted_iota(jnp.int32, (8, 128), 1)
    sub = lax.broadcasted_iota(jnp.int32, (8, 128), 0)
    other = (lane < 64) if start else (lane >= 64)
    rows = [w[8 * i:8 * i + 8, :] for i in range(8)]
    out = []
    for b in range(8):
        c = start + 8 * b
        bc = {i: [full(rows[i][:, c + k:c + k + 1]) for k in range(8)] for i in range(b, 8)}
        e = {(l, k): full(bc[b][k][l:l + 1, :]) for k in range(8) for l in range(k, 8)}
        u = [full(rows[b][k:k + 1, :]) for k in range(8)]
        done = jnp.zeros((8, 128), F32)
        for k in range(8):
            inv = 1.0 / e[k, k]
            for m in range(k + 1, 8):
                t = e[m, k] * inv
                for l in range(m, 8):
                    e[l, m] = e[l, m] - t * e[l, k]
                u[m] = u[m] - t * u[k]
                for i in range(b + 1, 8):
                    bc[i][m] = bc[i][m] - t * bc[i][k]
            scaled = u[k] * inv
            for i in range(b + 1, 8):
                rows[i] = rows[i] - bc[i][k] * scaled
            done = jnp.where(sub == k, u[k] * lax.rsqrt(e[k, k]), done)
        out.append(jnp.where(other, done, 0.0))
    return jnp.concatenate(out, axis=0)


def chol128(s, pump):
    r = lax.broadcasted_iota(jnp.int32, (64, 128), 0)
    c = lax.broadcasted_iota(jnp.int32, (64, 128), 1)
    low = jnp.where(c == r, 1.0, 0.0)
    high = jnp.where(c == r + 64, 1.0, 0.0)
    first = leaf(jnp.where(c < 64, s[:64], high), 0)
    pump(0)
    ma = pltpu.roll(first, 64, 1)
    l21 = mmt(jnp.where(c < 64, s[64:], 0.0), ma)
    s22 = mmt(l21, l21)
    z = jnp.zeros((64, 64), F32)
    s22 = jnp.concatenate([z, s22], axis=1)
    t = mm(l21, ma)
    second = leaf(jnp.where(c < 64, low, s[64:] - s22), 64)
    pump(1)
    low_part = mm(second[:, :64], high - t)
    return jnp.concatenate([ma, low_part], axis=0)


PARENTS = (
    (
        (-1, 0, 3, 0, 8, 9, 10, 11, 12, 8, 14, 8, 0, 12, 15, 12),
        (1, -1, 14, 15, 5, 1, 5, 6, 9, 13, 9, 15, 13, 1, 13, 14),
    ),
    (
        (-1, 5, 6, 7, 0, 4, 7, 4, 4, 5, 11, 7, 8, 9, 10, 11),
        (3, -1, 1, 2, 7, 6, 2, 3, 11, 10, 6, 10, 15, 14, 2, 3),
    ),
)


def neighbour(chip, direction):
    y, x = chip // 4, chip % 4
    if direction < 2:
        return y * 4 + (x + (1, 3)[direction]) % 4
    return (y + (1, 3)[direction - 2]) % 4 * 4 + x


def depth(core, panel, chip):
    parent = PARENTS[core][panel][chip]
    return 0 if parent < 0 else 1 + depth(core, panel, parent)


def handled_at(core, panel, chip):
    return depth(core, panel, chip) if chip in PARENTS[core][panel] else DEEPEST


def senders(core, panel, direction):
    parents = PARENTS[core][panel]
    return [n for n in range(16) if parents[neighbour(n, direction)] == n]


def panels_kernel(
    a_ref, w_ref, rows, slab, fac, leading, made, stage, lead, inv, low,
    local_sem, row_send, row_recv, slab_send, slab_recv,
    fac_send, fac_share, fac_give, fac_recv, lead_send, lead_recv,
):
    prow, pcol = lax.axis_index("prow"), lax.axis_index("pcol")
    z, core = prow // 2, prow % 2
    y, x = pcol // 4, pcol % 4
    both = jnp.logical_and
    is_root = both(core == 1, pcol == 0)
    gives_lead = (both(prow == 0, pcol == 0), both(prow == 1, pcol == 0), both(prow == 1, pcol == 1))

    def device(pz, pc, py, px):
        return {"prow": pz * 2 + pc, "pcol": py * 4 + px}

    def on_line(axis, step):
        if axis == "x":
            return device(z, core, y, (x + step) % 4)
        if axis == "y":
            return device(z, core, (y + step) % 4, x)
        return device((z + step) % 4, core, y, x)

    sibling = device(z, 1 - core, y, x)
    root = {"prow": z * 2 + 1, "pcol": 0}

    barrier = pltpu.get_barrier_semaphore()

    def greet(target):
        pl.semaphore_signal(barrier, 1, device_id=target, device_id_type=MESH)

    for axis in "xyz":
        for step in (1, 2, 3):
            greet(on_line(axis, step))
    greet(sibling)

    @pl.when(both(is_root, z > 0))
    def _():
        greet({"prow": 0, "pcol": 0})
        greet({"prow": 1, "pcol": 1})

    @pl.when(both(core == 0, pcol == 1))
    def _():
        greet(root)

    extra = jnp.where(is_root, 1, 0) + jnp.where(jnp.logical_or(gives_lead[0], gives_lead[2]), 3, 0)
    pl.semaphore_wait(barrier, 10 + extra)

    index = core * 16 + pcol
    gives = [[None] * 4 for _ in range(2)]
    for k in range(2):
        for d in range(4):
            flag = jnp.int32(0)
            for c in range(2):
                for n in senders(c, k, d):
                    flag = flag + jnp.where(index == c * 16 + n, 1, 0)
            gives[k][d] = flag == 1
    depths = []
    for k in range(2):
        value = jnp.int32(0)
        for c in range(2):
            for n in range(16):
                value = value + jnp.where(index == c * 16 + n, handled_at(c, k, n), 0)
        depths.append(value)
    targets = (on_line("x", 1), on_line("x", 3), on_line("y", 1), on_line("y", 3))

    def row_copy(src, k, d, first, count):
        piece = pl.ds(first, count)
        return pltpu.make_async_remote_copy(
            src_ref=src.at[piece, pl.ds(0, NB)] if src is a_ref else rows.at[k, piece, :],
            dst_ref=rows.at[k, piece, :],
            send_sem=row_send.at[k, d],
            recv_sem=row_recv.at[k, first // CHUNK if count == CHUNK else 0],
            device_id=targets[d],
            device_id_type=MESH,
        )

    on_ring = (core == 0, core == jnp.where(pcol == 0, 0, 1))
    along = (both(on_ring[0], z < 3), both(on_ring[1], z != 1))
    start_of_one = both(pcol == 0, z == 0)
    across = (on_ring[0], jnp.logical_or(both(start_of_one, core == 1), both(on_ring[1], jnp.logical_not(start_of_one))))
    slab_depths = (
        z + jnp.where(on_ring[0], 0, 1),
        (4 - z) % 4 + jnp.where(on_ring[1], 0, 1) + jnp.where(pcol == 0, 1, 0),
    )

    def slab_copy(src, s, slot, first, count):
        piece = pl.ds(first, count)
        step = 1 if s == 0 else 3
        return pltpu.make_async_remote_copy(
            src_ref=a_ref.at[piece, :] if src is a_ref else slab.at[s, piece, :],
            dst_ref=slab.at[s, piece, :],
            send_sem=slab_send.at[s, slot],
            recv_sem=slab_recv.at[s, first // STRIP if count == STRIP else 0],
            device_id=on_line("z", step) if slot == 0 else sibling,
            device_id_type=MESH,
        )

    def own_rows(k):
        return pltpu.make_async_copy(a_ref.at[:, pl.ds(0, NB)], rows.at[k], local_sem.at[k])

    def own_slab(s):
        return pltpu.make_async_copy(a_ref.at[pl.ds(0, NB), :], slab.at[s], local_sem.at[2 + s])

    def own_lead():
        return pltpu.make_async_copy(a_ref.at[pl.ds(0, NB), pl.ds(0, NB)], leading.at[1], local_sem.at[4])

    def own_block(i):
        piece = pl.ds(pl.multiple_of(i * NB, NB), NB)
        return pltpu.make_async_copy(a_ref.at[piece, :], w_ref.at[piece, :], local_sem.at[5 + i])

    def lead_copy(n, e, to_z):
        down, right, size = (0, 0, NB) if n == 1 else ((e + 1) // 2 * HALF, e // 2 * HALF, HALF)
        return pltpu.make_async_remote_copy(
            src_ref=a_ref.at[pl.ds(down, size), pl.ds(right, size)],
            dst_ref=leading.at[n, pl.ds(down, size), pl.ds(right, size)],
            send_sem=lead_send.at[n, e, to_z],
            recv_sem=lead_recv.at[n, e],
            device_id={"prow": 2 * to_z + 1, "pcol": 0},
            device_id_type=MESH,
        )

    def leads():
        for n in range(3):
            for e in range(1 if n == 1 else 3):
                for to_z in ((1, 3, 2) if n == 1 else (0, 1, 3, 2)):
                    yield n, e, to_z

    for n, e, to_z in leads():
        @pl.when(gives_lead[n])
        def _(n=n, e=e, to_z=to_z):
            lead_copy(n, e, to_z).start()

    @pl.when(gives_lead[1])
    def _():
        own_lead().start()

    for s in range(2):
        @pl.when(prow == s)
        def _(s=s):
            own_slab(s).start()

    for k in range(2):
        @pl.when(pcol == k)
        def _(k=k):
            own_rows(k).start()

    def send_chunk(src, k, i):
        for d in range(4):
            @pl.when(gives[k][d])
            def _(d=d):
                row_copy(src, k, d, i * CHUNK, CHUNK).start()

    def send_strip(src, s, j):
        @pl.when(along[s])
        def _():
            slab_copy(src, s, 0, j * STRIP, STRIP).start()

        @pl.when(across[s])
        def _():
            slab_copy(src, s, 1, j * STRIP, STRIP).start()

    def fac_block(ref, part, e):
        i, j = (e // 2, e % 2) if part == 1 else ((e + 1) // 2, e // 2)
        if not isinstance(e, int):
            i, j = pl.multiple_of(i * HALF, HALF), pl.multiple_of(j * HALF, HALF)
        else:
            i, j = i * HALF, j * HALF
        return ref.at[part, pl.ds(i, HALF), pl.ds(j, HALF)]

    def fac_copy(src, part, e, send_sem, target):
        return pltpu.make_async_remote_copy(
            src_ref=fac_block(src, part, e),
            dst_ref=fac_block(fac, part, e),
            send_sem=send_sem,
            recv_sem=fac_recv.at[FIRST_MESSAGE[part] + e],
            device_id=target,
            device_id_type=MESH,
        )

    def each_fac(part, k, act):
        e = core * 2 + k
        for d in range(4):
            @pl.when(gives[k][d])
            def _(d=d):
                act(fac_copy(fac, part, e, fac_send.at[part, k, d], targets[d]))
        act(fac_copy(fac, part, e, fac_share.at[part, k], sibling))

    def root_fac(part, act):
        for e, target in ((0, sibling), (1, {"prow": z * 2, "pcol": 1}), (3, {"prow": z * 2 + 1, "pcol": 1})):
            if e < BLOCKS[part]:
                act(fac_copy(made, part, e, fac_give.at[part, e], target))

    def begin(copy):
        copy.start()

    def finish(copy):
        copy.wait_send()

    def give_part(part):
        root_fac(part, begin)
        i, j = (1, 0) if part == 1 else (1, 1)
        span = (part, pl.ds(i * HALF, HALF), pl.ds(j * HALF, HALF))
        fac[span] = made[span]
        each_fac(part, 0, begin)

    def pass_rows(tick):
        for k in range(2):
            n = tick - LAG * depths[k]
            skips = jnp.int32(0)
            special = n < 0
            for place in PLACES:
                skips = skips + jnp.where(n > place, 1, 0)
                special = jnp.logical_or(special, n == place)
            i = n - skips
            here = both(jnp.logical_not(special), n < ITEMS)
            mine = both(here, pcol == k)
            if k == 0:
                mine = both(mine, jnp.logical_not(is_root))

            @pl.when(both(here, pcol != k))
            def _(k=k, i=i):
                row_copy(None, k, 0, i * CHUNK, CHUNK).wait_recv()
                send_chunk(None, k, i)

            @pl.when(mine)
            def _(k=k, i=i):
                send_chunk(a_ref, k, i)

            for part, place in enumerate(PLACES):
                now = both(n == place, core * 2 + k < BLOCKS[part])
                if k == 0:
                    now = both(now, jnp.logical_not(is_root))

                @pl.when(now)
                def _(k=k, part=part):
                    fac_copy(fac, part, core * 2 + k, fac_share.at[part, k], sibling).wait_recv()
                    each_fac(part, k, begin)

    def pass_slab(tick):
        for s in range(2):
            j = tick - SLAB_TICK - LAG * slab_depths[s]
            here = both(j >= 0, j < STRIPS)

            @pl.when(both(here, prow != s))
            def _(s=s, j=j):
                slab_copy(None, s, 0, j * STRIP, STRIP).wait_recv()
                send_strip(None, s, j)

            @pl.when(both(both(tick < STRIPS, prow == s), jnp.logical_not(is_root)))
            def _(s=s):
                send_strip(a_ref, s, tick)

    for part in (0, 2):
        fac[part, 0:HALF, HALF:NB] = jnp.zeros((HALF, HALF), F32)

    @pl.when(is_root)
    def _():
        def pump(first, count):
            def one(i, carry):
                @pl.when(i < CHUNKS)
                def _():
                    send_chunk(a_ref, 0, i)

                return carry

            lax.fori_loop(first, first + count, one, 0)

        pump(0, AHEAD)

        @pl.when(prow == 1)
        def _():
            def one(j, carry):
                send_strip(a_ref, 1, j)
                return carry

            lax.fori_loop(0, STRIPS, one, 0)

        lead_copy(0, 0, z).wait_recv()
        lead[...] = leading[0, 0:HALF, 0:HALF]

        def panel(k, carry):
            def half(h, inner):
                inv[h] = chol128(lead[...], lambda n: pump(AHEAD + (4 * k + 2 * h + n) * PUMP, PUMP))

                @pl.when(h == 0)
                def _():
                    @pl.when(k == 0)
                    def _():
                        for e in (1, 2):
                            lead_copy(0, e, z).wait_recv()
                        stage[HALF:NB, :] = leading[0, HALF:NB, :]

                    low[...] = mmt(stage[HALF:NB, 0:HALF], inv[0])
                    lead[...] = stage[HALF:NB, HALF:NB] - mmt(low[...], low[...])

                return inner

            lax.fori_loop(0, 2, half, 0)
            made[2 * k, 0:HALF, 0:HALF] = inv[0]
            made[2 * k, 0:HALF, HALF:NB] = jnp.zeros((HALF, HALF), F32)
            made[2 * k, HALF:NB, HALF:NB] = inv[1]
            made[2 * k, HALF:NB, 0:HALF] = -mm(inv[1], mm(low[...], inv[0]))

            @pl.when(k == 0)
            def _():
                give_part(0)

                @pl.when(prow == 1)
                def _():
                    own_lead().wait()

                @pl.when(prow != 1)
                def _():
                    lead_copy(1, 0, z).wait_recv()

                made[1] = mmt(leading[1], made[0])
                give_part(1)
                for e in range(3):
                    lead_copy(2, e, z).wait_recv()
                square = mmt(made[1], made[1])
                lead[...] = leading[2, 0:HALF, 0:HALF] - square[0:HALF, 0:HALF]
                stage[HALF:NB, :] = leading[2, HALF:NB, :] - square[HALF:NB, :]

            @pl.when(k == 1)
            def _():
                give_part(2)

            return carry

        lax.fori_loop(0, 2, panel, 0)

    for k in range(2):
        @pl.when(pcol == k)
        def _(k=k):
            own_rows(k).wait()

    for s in range(2):
        @pl.when(prow == s)
        def _(s=s):
            own_slab(s).wait()

    def step(tick, carry):
        pass_rows(tick)
        pass_slab(tick)

        @pl.when(both(tick % 2 == 1, tick < 2 * (ROWS // NB)))
        def _():
            own_block(tick // 2).start()

        return carry

    lax.fori_loop(0, TICKS, step, 0)

    for part in range(3):
        for k in range(2):
            other = (1 - core) * 2 + k

            @pl.when(other < BLOCKS[part])
            def _(part=part, k=k, other=other):
                fac_copy(fac, part, other, fac_share.at[part, k], sibling).wait_recv()

    def block_here(i, carry):
        own_block(i).wait()
        return carry

    lax.fori_loop(0, ROWS // NB, block_here, 0)

    for k in range(2):
        for d in range(4):
            @pl.when(gives[k][d])
            def _(k=k, d=d):
                row_copy(None, k, d, 0, ROWS).wait_send()

    for s in range(2):
        for slot, condition in enumerate((along[s], across[s])):
            @pl.when(condition)
            def _(s=s, slot=slot):
                slab_copy(None, s, slot, 0, NB).wait_send()

    for part in range(3):
        for k in range(2):
            @pl.when(core * 2 + k < BLOCKS[part])
            def _(part=part, k=k):
                each_fac(part, k, finish)

        @pl.when(is_root)
        def _(part=part):
            root_fac(part, finish)

    for n, e, to_z in leads():
        @pl.when(gives_lead[n])
        def _(n=n, e=e, to_z=to_z):
            lead_copy(n, e, to_z).wait_send()


def make_panels(matrix):
    dma = pltpu.SemaphoreType.DMA
    vmem = pl.BlockSpec(memory_space=pltpu.VMEM)
    return pl.pallas_call(
        panels_kernel,
        out_shape=(
            jax.ShapeDtypeStruct((ROWS, COLS), F32),
            jax.ShapeDtypeStruct((2, ROWS, NB), F32),
            jax.ShapeDtypeStruct((2, NB, COLS), F32),
            jax.ShapeDtypeStruct((3, NB, NB), F32),
        ),
        in_specs=[pl.BlockSpec(memory_space=pl.ANY)],
        out_specs=(vmem, vmem, vmem, vmem),
        scratch_shapes=[
            pltpu.VMEM((3, NB, NB), F32),
            pltpu.VMEM((3, NB, NB), F32),
            pltpu.VMEM((NB, NB), F32),
            pltpu.VMEM((HALF, HALF), F32),
            pltpu.VMEM((2, HALF, HALF), F32),
            pltpu.VMEM((HALF, HALF), F32),
            dma((5 + ROWS // NB,)),
            dma((2, 4)),
            dma((2, CHUNKS)),
            dma((2, 2)),
            dma((2, STRIPS)),
            dma((3, 2, 4)),
            dma((3, 2)),
            dma((3, 4)),
            dma((sum(BLOCKS),)),
            dma((3, 3, 4)),
            dma((3, 3)),
        ],
        compiler_params=pltpu.CompilerParams(
            collective_id=0, has_side_effects=True, vmem_limit_bytes=32 * 2**20
        ),
        cost_estimate=pl.CostEstimate(flops=2**30, bytes_accessed=2**24, transcendentals=0),
        name="panels",
    )(matrix)


def update_kernel(place, w_ref, rows, slab, fac, out_ref, c_high, c_low, f_split):
    i = pl.program_id(0)

    @pl.when(i == 0)
    def _():
        for part in range(3):
            f_split[part, 0], f_split[part, 1] = split(fac[part])

        def columns(j, carry):
            tile = pl.ds(pl.multiple_of(j * NB, NB), NB)
            first = three(f_split[0, 0], f_split[0, 1], *split(slab[0, :, tile]))
            high, low = split(first)
            c_high[0:NB, tile] = high
            c_low[0:NB, tile] = low
            rest = slab[1, :, tile] - three(f_split[1, 0], f_split[1, 1], high, low)
            high, low = split(three(f_split[2, 0], f_split[2, 1], *split(rest)))
            c_high[NB:2 * NB, tile] = high
            c_low[NB:2 * NB, tile] = low
            return carry

        lax.fori_loop(0, COLS // NB, columns, 0)

    prow, pcol = place[0], place[1]
    row_block = i * 8 + prow
    block = pl.ds(pl.multiple_of(i * NB, NB), NB)
    first = three_t(*split(rows[0, block, :]), f_split[0, 0], f_split[0, 1])
    first_high, first_low = split(first)
    rest = rows[1, block, :] - three_t(first_high, first_low, f_split[1, 0], f_split[1, 1])
    second = three_t(*split(rest), f_split[2, 0], f_split[2, 1])
    second_high, second_low = split(second)
    high = jnp.concatenate([first_high, second_high], axis=1)
    low = jnp.concatenate([first_low, second_low], axis=1)
    out_ref[...] = w_ref[block, :] - three(high, low, c_high[...], c_low[...])

    @pl.when(row_block < 2)
    def _():
        out_ref[...] = jnp.zeros((NB, COLS), F32)

    down = lax.broadcasted_iota(jnp.int32, (NB, NB), 0)
    right = lax.broadcasted_iota(jnp.int32, (NB, NB), 1)
    for k, panel in enumerate((first, second)):
        @pl.when(both_true(pcol == k, row_block >= k))
        def _(k=k, panel=panel):
            keep = jnp.logical_or(row_block > k, right <= down)
            out_ref[:, 0:NB] = jnp.where(keep, panel, 0.0)


def both_true(a, b):
    return jnp.logical_and(a, b)


def update(matrix, rows, slab, fac):
    place = jnp.stack([lax.axis_index("prow"), lax.axis_index("pcol")]).astype(jnp.int32)
    vmem = pl.BlockSpec(memory_space=pltpu.VMEM)
    return pl.pallas_call(
        update_kernel,
        out_shape=jax.ShapeDtypeStruct((ROWS, COLS), F32),
        grid=(ROWS // NB,),
        in_specs=[pl.BlockSpec(memory_space=pltpu.SMEM), vmem, vmem, vmem, vmem],
        out_specs=pl.BlockSpec((NB, COLS), lambda i: (i, 0)),
        scratch_shapes=[
            pltpu.VMEM((2 * NB, COLS), BF16),
            pltpu.VMEM((2 * NB, COLS), BF16),
            pltpu.VMEM((3, 2, NB, NB), BF16),
        ],
        compiler_params=pltpu.CompilerParams(vmem_limit_bytes=32 * 2**20),
        cost_estimate=pl.CostEstimate(
            flops=2 * 3 * ROWS * COLS * 2 * NB, bytes_accessed=2**24, transcendentals=0
        ),
        name="update",
    )(place, matrix, rows, slab, fac)


def body(matrix):
    return update(*make_panels(matrix))


def solution(mesh):
    spec = P("prow", "pcol")
    return jax.shard_map(body, mesh=mesh, in_specs=(spec,), out_specs=spec, check_vma=False)
```

time: 100 us -> 88.8 us (0.89)
  the two profiles are of different devices: /device:TPU:14 before, /device:TPU:45 now
where the time goes in v3:
time: 88.8 us; the launch traced here: 88.7 us
  Pallas kernels  88.6 us (100%)
    pallas_call x1, Pallas kernels, make_panels(): pl.pallas_call(panels_kernel, out_shape=(jax.ShapeDtypeStruct((ROWS, COLS...  61.3 us
    pallas_call x1, Pallas kernels, update(): pl.pallas_call(update_kernel, out_shape=jax.ShapeDtypeStruct((ROWS, COLS)...  27.3 us

profile of v3, /device:TPU:45, one launch (start us, length us, event | category | flops | bytes accessed | tf_op | source)
XLA Modules:
  0.0 88.7 jit_solution(5950064770840881907)
XLA Ops:
  0.0 0.1 pad_add_fusion.place
  0.1 61.3 %panels.1 = (f32[2560,1280]{1,0:T(8,128)S(1)}, f32[2,2560,256]{2,1,0:T(8,128)S(1)}, f32[2,256,1280]{2,1,0:T(8,128)S(1)}, f32[3,256,256]{2,1,0:T(8,128)S(1)}) custom-call(f32[2560,1280]{1,0:T(8,128)} %a_ref.1), custom_call_target="tpu_custom_call" | custom-call | flops 1073741824 | bytes 16777216 | tf_op jit(solution)/shard_map/panels/pallas_call | solution.py:538
  61.4 27.3 %update.1 = f32[2560,1280]{1,0:T(8,128)} custom-call(s32[2]{0:T(128)S(1)} %pad_add_fusion.place, f32[2560,1280]{1,0:T(8,128)S(1)} %get-tuple-element.9.w_ref, f32[2,2560,256]{2,1,0:T(8,128)S(1)} %get-tuple-element.10.rows, f32[2,256,1280]{2,1,0:T(8,128)S(1)} %get-tuple-element.11.slab, f32[3,256,256]{2,1,0:T(8,128)S(1)} %get-tuple-element.12.fac), custom_call_target="tpu_custom_call" | custom-call | flops 10066329600 | bytes 16777216 | tf_op jit(solution)/shard_map/update/pallas_call | solution.py:629

commit v4 on v3

--- a/solution.py
+++ b/solution.py
@@ -19,12 +19,16 @@
 STRIPS = NB // STRIP
 BLOCKS = (3, 4, 3)
 FIRST_MESSAGE = (0, 3, 7)
-PLACES = (25, 29, 42)
+PLACES = (27, 30, 42)
 ITEMS = CHUNKS + len(PLACES)
 LAG = 4
 DEEPEST = 5
 TICKS = ITEMS + LAG * DEEPEST
 SLAB_TICK = 12
+FIRST_WORK = PLACES[0] + LAG * DEEPEST + 1
+ROWS_WORK = TICKS - ROWS // NB
+COLUMN_BLOCKS = COLS // NB
+ROW_BLOCKS = ROWS // NB
 AHEAD = 6
 PUMP = 5
 
@@ -138,7 +142,7 @@
 
 
 def panels_kernel(
-    a_ref, w_ref, rows, slab, fac, leading, made, stage, lead, inv, low,
+    a_ref, w_ref, r_high, r_low, c_high, c_low, rows, slab, fac, fac_split, rest, leading, made, stage, lead, inv, low,
     local_sem, row_send, row_recv, slab_send, slab_recv,
     fac_send, fac_share, fac_give, fac_recv, lead_send, lead_recv,
 ):
@@ -244,7 +248,7 @@
         return pltpu.make_async_copy(a_ref.at[pl.ds(0, NB), pl.ds(0, NB)], leading.at[1], local_sem.at[4])
 
     def own_block(i):
-        piece = pl.ds(pl.multiple_of(i * NB, NB), NB)
+        piece = pl.ds(pl.multiple_of(i * CHUNK, CHUNK), CHUNK)
         return pltpu.make_async_copy(a_ref.at[piece, :], w_ref.at[piece, :], local_sem.at[5 + i])
 
     def lead_copy(n, e, to_z):
@@ -478,31 +482,76 @@
         def _(s=s):
             own_slab(s).wait()
 
-    def step(tick, carry):
+    def step(tick):
         pass_rows(tick)
         pass_slab(tick)
 
-        @pl.when(both(tick % 2 == 1, tick < 2 * (ROWS // NB)))
+    def early(tick, carry):
+        step(tick)
+
+        @pl.when(tick < CHUNKS)
         def _():
-            own_block(tick // 2).start()
+            own_block(tick).start()
 
         return carry
 
-    lax.fori_loop(0, TICKS, step, 0)
-
-    for part in range(3):
+    def part_here(part):
         for k in range(2):
             other = (1 - core) * 2 + k
 
             @pl.when(other < BLOCKS[part])
-            def _(part=part, k=k, other=other):
+            def _(k=k, other=other):
                 fac_copy(fac, part, other, fac_share.at[part, k], sibling).wait_recv()
+
+        fac_split[part, 0], fac_split[part, 1] = split(fac[part])
+
+    def first_columns(j, carry):
+        step(FIRST_WORK + j)
+        tile = pl.ds(pl.multiple_of(j * NB, NB), NB)
+        high, low_part = split(three(fac_split[0, 0], fac_split[0, 1], *split(slab[0, :, tile])))
+        c_high[0:NB, tile] = high
+        c_low[0:NB, tile] = low_part
+        return carry
+
+    def first_rows(i, carry):
+        step(ROWS_WORK + i)
+        block = pl.ds(pl.multiple_of(i * NB, NB), NB)
+        first = three_t(*split(rows[0, block, :]), fac_split[0, 0], fac_split[0, 1])
+        high, low_part = split(first)
+        r_high[block, 0:NB] = high
+        r_low[block, 0:NB] = low_part
+        rest[block, :] = rows[1, block, :] - three_t(high, low_part, fac_split[1, 0], fac_split[1, 1])
+        return carry
+
+    lax.fori_loop(0, FIRST_WORK, early, 0)
+    part_here(0)
+    lax.fori_loop(0, COLUMN_BLOCKS, first_columns, 0)
+    lax.fori_loop(FIRST_WORK + COLUMN_BLOCKS, ROWS_WORK, early, 0)
+    part_here(1)
+    lax.fori_loop(0, ROW_BLOCKS, first_rows, 0)
+    part_here(2)
+
+    for j in range(COLUMN_BLOCKS):
+        tile = pl.ds(j * NB, NB)
+        left = slab[1, :, tile] - three(fac_split[1, 0], fac_split[1, 1], c_high[0:NB, tile], c_low[0:NB, tile])
+        high, low_part = split(three(fac_split[2, 0], fac_split[2, 1], *split(left)))
+        c_high[NB:2 * NB, tile] = high
+        c_low[NB:2 * NB, tile] = low_part
+
+    def second_rows(i, carry):
+        block = pl.ds(pl.multiple_of(i * 2 * NB, 2 * NB), 2 * NB)
+        high, low_part = split(three_t(*split(rest[block, :]), fac_split[2, 0], fac_split[2, 1]))
+        r_high[block, NB:2 * NB] = high
+        r_low[block, NB:2 * NB] = low_part
+        return carry
+
+    lax.fori_loop(0, ROW_BLOCKS // 2, second_rows, 0)
 
     def block_here(i, carry):
         own_block(i).wait()
         return carry
 
-    lax.fori_loop(0, ROWS // NB, block_here, 0)
+    lax.fori_loop(0, CHUNKS, block_here, 0)
 
     for k in range(2):
         for d in range(4):
@@ -539,20 +588,26 @@
         panels_kernel,
         out_shape=(
             jax.ShapeDtypeStruct((ROWS, COLS), F32),
-            jax.ShapeDtypeStruct((2, ROWS, NB), F32),
-            jax.ShapeDtypeStruct((2, NB, COLS), F32),
-            jax.ShapeDtypeStruct((3, NB, NB), F32),
+            jax.ShapeDtypeStruct((ROWS, 2 * NB), BF16),
+            jax.ShapeDtypeStruct((ROWS, 2 * NB), BF16),
+            jax.ShapeDtypeStruct((2 * NB, COLS), BF16),
+            jax.ShapeDtypeStruct((2 * NB, COLS), BF16),
         ),
         in_specs=[pl.BlockSpec(memory_space=pl.ANY)],
-        out_specs=(vmem, vmem, vmem, vmem),
+        out_specs=(vmem, vmem, vmem, vmem, vmem),
         scratch_shapes=[
+            pltpu.VMEM((2, ROWS, NB), F32),
+            pltpu.VMEM((2, NB, COLS), F32),
+            pltpu.VMEM((3, NB, NB), F32),
+            pltpu.VMEM((3, 2, NB, NB), BF16),
+            pltpu.VMEM((ROWS, NB), F32),
             pltpu.VMEM((3, NB, NB), F32),
             pltpu.VMEM((3, NB, NB), F32),
             pltpu.VMEM((NB, NB), F32),
             pltpu.VMEM((HALF, HALF), F32),
             pltpu.VMEM((2, HALF, HALF), F32),
             pltpu.VMEM((HALF, HALF), F32),
-            dma((5 + ROWS // NB,)),
+            dma((5 + CHUNKS,)),
             dma((2, 4)),
             dma((2, CHUNKS)),
             dma((2, 2)),
@@ -572,39 +627,12 @@
     )(matrix)
 
 
-def update_kernel(place, w_ref, rows, slab, fac, out_ref, c_high, c_low, f_split):
+def update_kernel(place, w_ref, r_high, r_low, c_high, c_low, out_ref):
     i = pl.program_id(0)
-
-    @pl.when(i == 0)
-    def _():
-        for part in range(3):
-            f_split[part, 0], f_split[part, 1] = split(fac[part])
-
-        def columns(j, carry):
-            tile = pl.ds(pl.multiple_of(j * NB, NB), NB)
-            first = three(f_split[0, 0], f_split[0, 1], *split(slab[0, :, tile]))
-            high, low = split(first)
-            c_high[0:NB, tile] = high
-            c_low[0:NB, tile] = low
-            rest = slab[1, :, tile] - three(f_split[1, 0], f_split[1, 1], high, low)
-            high, low = split(three(f_split[2, 0], f_split[2, 1], *split(rest)))
-            c_high[NB:2 * NB, tile] = high
-            c_low[NB:2 * NB, tile] = low
-            return carry
-
-        lax.fori_loop(0, COLS // NB, columns, 0)
-
     prow, pcol = place[0], place[1]
     row_block = i * 8 + prow
     block = pl.ds(pl.multiple_of(i * NB, NB), NB)
-    first = three_t(*split(rows[0, block, :]), f_split[0, 0], f_split[0, 1])
-    first_high, first_low = split(first)
-    rest = rows[1, block, :] - three_t(first_high, first_low, f_split[1, 0], f_split[1, 1])
-    second = three_t(*split(rest), f_split[2, 0], f_split[2, 1])
-    second_high, second_low = split(second)
-    high = jnp.concatenate([first_high, second_high], axis=1)
-    low = jnp.concatenate([first_low, second_low], axis=1)
-    out_ref[...] = w_ref[block, :] - three(high, low, c_high[...], c_low[...])
+    out_ref[...] = w_ref[block, :] - three(r_high[block, :], r_low[block, :], c_high[...], c_low[...])
 
     @pl.when(row_block < 2)
     def _():
@@ -612,37 +640,30 @@
 
     down = lax.broadcasted_iota(jnp.int32, (NB, NB), 0)
     right = lax.broadcasted_iota(jnp.int32, (NB, NB), 1)
-    for k, panel in enumerate((first, second)):
-        @pl.when(both_true(pcol == k, row_block >= k))
-        def _(k=k, panel=panel):
+    for k in range(2):
+        @pl.when(jnp.logical_and(pcol == k, row_block >= k))
+        def _(k=k):
+            panel = pl.ds(k * NB, NB)
+            value = r_high[block, panel].astype(F32) + r_low[block, panel].astype(F32)
             keep = jnp.logical_or(row_block > k, right <= down)
-            out_ref[:, 0:NB] = jnp.where(keep, panel, 0.0)
-
-
-def both_true(a, b):
-    return jnp.logical_and(a, b)
-
-
-def update(matrix, rows, slab, fac):
+            out_ref[:, 0:NB] = jnp.where(keep, value, 0.0)
+
+
+def update(matrix, *panels):
     place = jnp.stack([lax.axis_index("prow"), lax.axis_index("pcol")]).astype(jnp.int32)
     vmem = pl.BlockSpec(memory_space=pltpu.VMEM)
     return pl.pallas_call(
         update_kernel,
         out_shape=jax.ShapeDtypeStruct((ROWS, COLS), F32),
         grid=(ROWS // NB,),
-        in_specs=[pl.BlockSpec(memory_space=pltpu.SMEM), vmem, vmem, vmem, vmem],
+        in_specs=[pl.BlockSpec(memory_space=pltpu.SMEM)] + [vmem] * 5,
         out_specs=pl.BlockSpec((NB, COLS), lambda i: (i, 0)),
-        scratch_shapes=[
-            pltpu.VMEM((2 * NB, COLS), BF16),
-            pltpu.VMEM((2 * NB, COLS), BF16),
-            pltpu.VMEM((3, 2, NB, NB), BF16),
-        ],
         compiler_params=pltpu.CompilerParams(vmem_limit_bytes=32 * 2**20),
         cost_estimate=pl.CostEstimate(
             flops=2 * 3 * ROWS * COLS * 2 * NB, bytes_accessed=2**24, transcendentals=0
         ),
         name="update",
-    )(place, matrix, rows, slab, fac)
+    )(place, matrix, *panels)
 
 
 def body(matrix):

time: 88.8 us -> 81.5 us (0.918)
  the two profiles are of different devices: /device:TPU:45 before, /device:TPU:65 now
where the time goes in v4:
time: 81.5 us; the launch traced here: 81.3 us
  Pallas kernels  81.3 us (100%)
    pallas_call x1, Pallas kernels, make_panels(): pl.pallas_call(panels_kernel, out_shape=(jax.ShapeDtypeStruct((ROWS, COLS...  67.1 us
    pallas_call x1, Pallas kernels, update(): pl.pallas_call(update_kernel, out_shape=jax.ShapeDtypeStruct((ROWS, COLS)...  14.2 us

profile of v4, /device:TPU:65, one launch (start us, length us, event | category | flops | bytes accessed | tf_op | source)
XLA Modules:
  0.0 81.3 jit_solution(3196882049151762365)
XLA Ops:
  0.0 0.1 pad_add_fusion.place
  0.1 67.1 %panels.1 = (f32[2560,1280]{1,0:T(8,128)S(1)}, bf16[2560,512]{1,0:T(8,128)(2,1)S(1)}, bf16[2560,512]{1,0:T(8,128)(2,1)S(1)}, bf16[512,1280]{1,0:T(8,128)(2,1)S(1)}, bf16[512,1280]{1,0:T(8,128)(2,1)S(1)}) custom-call(f32[2560,1280]{1,0:T(8,128)} %a_ref.1), custom_call_target="tpu_custom_call" | custom-call | flops 1073741824 | bytes 16777216 | tf_op jit(solution)/shard_map/panels/pallas_call | solution.py:587
  67.2 14.2 %update.1 = f32[2560,1280]{1,0:T(8,128)} custom-call(s32[2]{0:T(128)S(1)} %pad_add_fusion.place, f32[2560,1280]{1,0:T(8,128)S(1)} %get-tuple-element.10.w_ref, bf16[2560,512]{1,0:T(8,128)(2,1)S(1)} %get-tuple-element.11.r_high, bf16[2560,512]{1,0:T(8,128)(2,1)S(1)} %get-tuple-element.12.r_low, bf16[512,1280]{1,0:T(8,128)(2,1)S(1)} %get-tuple-element.13.c_high, ...), custom_call_target="tpu_custom_call" | custom-call | flops 10066329600 | bytes 16777216 | tf_op jit(solution)/shard_map/update/pallas_call | solution.py:655

commit v5 on v4

--- a/solution.py
+++ b/solution.py
@@ -19,13 +19,14 @@
 STRIPS = NB // STRIP
 BLOCKS = (3, 4, 3)
 FIRST_MESSAGE = (0, 3, 7)
-PLACES = (27, 30, 42)
+PLACES = (25, 27, 42)
 ITEMS = CHUNKS + len(PLACES)
 LAG = 4
 DEEPEST = 5
 TICKS = ITEMS + LAG * DEEPEST
 SLAB_TICK = 12
-FIRST_WORK = PLACES[0] + LAG * DEEPEST + 1
+OWN_TICK = 44
+FIRST_WORK = PLACES[1] + LAG * DEEPEST + 1
 ROWS_WORK = TICKS - ROWS // NB
 COLUMN_BLOCKS = COLS // NB
 ROW_BLOCKS = ROWS // NB
@@ -142,7 +143,7 @@
 
 
 def panels_kernel(
-    a_ref, w_ref, r_high, r_low, c_high, c_low, rows, slab, fac, fac_split, rest, leading, made, stage, lead, inv, low,
+    a_ref, w_ref, r_high, r_low, c_high, c_low, rows, slab, fac, fac_split, rest, left, leading, made, stage, lead, inv, low,
     local_sem, row_send, row_recv, slab_send, slab_recv,
     fac_send, fac_share, fac_give, fac_recv, lead_send, lead_recv,
 ):
@@ -165,6 +166,9 @@
 
     sibling = device(z, 1 - core, y, x)
     root = {"prow": z * 2 + 1, "pcol": 0}
+
+    def own_block():
+        return pltpu.make_async_copy(a_ref, w_ref, local_sem.at[5])
 
     barrier = pltpu.get_barrier_semaphore()
 
@@ -247,10 +251,6 @@
     def own_lead():
         return pltpu.make_async_copy(a_ref.at[pl.ds(0, NB), pl.ds(0, NB)], leading.at[1], local_sem.at[4])
 
-    def own_block(i):
-        piece = pl.ds(pl.multiple_of(i * CHUNK, CHUNK), CHUNK)
-        return pltpu.make_async_copy(a_ref.at[piece, :], w_ref.at[piece, :], local_sem.at[5 + i])
-
     def lead_copy(n, e, to_z):
         down, right, size = (0, 0, NB) if n == 1 else ((e + 1) // 2 * HALF, e // 2 * HALF, HALF)
         return pltpu.make_async_remote_copy(
@@ -431,10 +431,16 @@
                     def _():
                         for e in (1, 2):
                             lead_copy(0, e, z).wait_recv()
-                        stage[HALF:NB, :] = leading[0, HALF:NB, :]
-
-                    low[...] = mmt(stage[HALF:NB, 0:HALF], inv[0])
-                    lead[...] = stage[HALF:NB, HALF:NB] - mmt(low[...], low[...])
+                        stage[...] = leading[0, HALF:NB, :]
+
+                    @pl.when(k == 1)
+                    def _():
+                        for e in (1, 2):
+                            lead_copy(2, e, z).wait_recv()
+                        stage[...] = leading[2, HALF:NB, :] - mmt(made[1, HALF:NB, :], made[1])
+
+                    low[...] = mmt(stage[:, 0:HALF], inv[0])
+                    lead[...] = stage[:, HALF:NB] - mmt(low[...], low[...])
 
                 return inner
 
@@ -457,12 +463,10 @@
                     lead_copy(1, 0, z).wait_recv()
 
                 made[1] = mmt(leading[1], made[0])
+                lead_copy(2, 0, z).wait_recv()
+                top = made[1, 0:HALF, :]
+                lead[...] = leading[2, 0:HALF, 0:HALF] - mmt(top, top)
                 give_part(1)
-                for e in range(3):
-                    lead_copy(2, e, z).wait_recv()
-                square = mmt(made[1], made[1])
-                lead[...] = leading[2, 0:HALF, 0:HALF] - square[0:HALF, 0:HALF]
-                stage[HALF:NB, :] = leading[2, HALF:NB, :] - square[HALF:NB, :]
 
             @pl.when(k == 1)
             def _():
@@ -489,9 +493,9 @@
     def early(tick, carry):
         step(tick)
 
-        @pl.when(tick < CHUNKS)
+        @pl.when(tick == OWN_TICK)
         def _():
-            own_block(tick).start()
+            own_block().start()
 
         return carry
 
@@ -511,6 +515,7 @@
         high, low_part = split(three(fac_split[0, 0], fac_split[0, 1], *split(slab[0, :, tile])))
         c_high[0:NB, tile] = high
         c_low[0:NB, tile] = low_part
+        left[:, tile] = slab[1, :, tile] - three(fac_split[1, 0], fac_split[1, 1], high, low_part)
         return carry
 
     def first_rows(i, carry):
@@ -523,18 +528,42 @@
         rest[block, :] = rows[1, block, :] - three_t(high, low_part, fac_split[1, 0], fac_split[1, 1])
         return carry
 
-    lax.fori_loop(0, FIRST_WORK, early, 0)
+    @pl.when(jnp.logical_not(is_root))
+    def _():
+        lax.fori_loop(0, FIRST_WORK, early, 0)
+
+    @pl.when(is_root)
+    def _():
+        own_block().start()
+
+        def chunk_here(i, carry):
+            row_copy(None, 1, 0, i * CHUNK, CHUNK).wait_recv()
+            return carry
+
+        first_ticks = FIRST_WORK - LAG * DEEPEST
+        lax.fori_loop(0, first_ticks - sum(place < first_ticks for place in PLACES), chunk_here, 0)
+        fac_copy(fac, 1, 3, fac_share.at[1, 1], sibling).wait_recv()
+        each_fac(1, 1, begin)
+
+        for s in range(2):
+            @pl.when(prow != s)
+            def _(s=s):
+                def strip_here(j, carry):
+                    slab_copy(None, s, 0, j * STRIP, STRIP).wait_recv()
+                    return carry
+
+                lax.fori_loop(0, STRIPS, strip_here, 0)
+
     part_here(0)
+    part_here(1)
     lax.fori_loop(0, COLUMN_BLOCKS, first_columns, 0)
     lax.fori_loop(FIRST_WORK + COLUMN_BLOCKS, ROWS_WORK, early, 0)
-    part_here(1)
     lax.fori_loop(0, ROW_BLOCKS, first_rows, 0)
     part_here(2)
 
     for j in range(COLUMN_BLOCKS):
         tile = pl.ds(j * NB, NB)
-        left = slab[1, :, tile] - three(fac_split[1, 0], fac_split[1, 1], c_high[0:NB, tile], c_low[0:NB, tile])
-        high, low_part = split(three(fac_split[2, 0], fac_split[2, 1], *split(left)))
+        high, low_part = split(three(fac_split[2, 0], fac_split[2, 1], *split(left[:, tile])))
         c_high[NB:2 * NB, tile] = high
         c_low[NB:2 * NB, tile] = low_part
 
@@ -547,11 +576,7 @@
 
     lax.fori_loop(0, ROW_BLOCKS // 2, second_rows, 0)
 
-    def block_here(i, carry):
-        own_block(i).wait()
-        return carry
-
-    lax.fori_loop(0, CHUNKS, block_here, 0)
+    own_block().wait()
 
     for k in range(2):
         for d in range(4):
@@ -601,13 +626,14 @@
             pltpu.VMEM((3, NB, NB), F32),
             pltpu.VMEM((3, 2, NB, NB), BF16),
             pltpu.VMEM((ROWS, NB), F32),
+            pltpu.VMEM((NB, COLS), F32),
             pltpu.VMEM((3, NB, NB), F32),
             pltpu.VMEM((3, NB, NB), F32),
-            pltpu.VMEM((NB, NB), F32),
+            pltpu.VMEM((HALF, NB), F32),
             pltpu.VMEM((HALF, HALF), F32),
             pltpu.VMEM((2, HALF, HALF), F32),
             pltpu.VMEM((HALF, HALF), F32),
-            dma((5 + CHUNKS,)),
+            dma((6,)),
             dma((2, 4)),
             dma((2, CHUNKS)),
             dma((2, 2)),
@@ -627,9 +653,9 @@
     )(matrix)
 
 
-def update_kernel(place, w_ref, r_high, r_low, c_high, c_low, out_ref):
+def update_kernel(w_ref, r_high, r_low, c_high, c_low, out_ref):
     i = pl.program_id(0)
-    prow, pcol = place[0], place[1]
+    prow, pcol = lax.axis_index("prow"), lax.axis_index("pcol")
     row_block = i * 8 + prow
     block = pl.ds(pl.multiple_of(i * NB, NB), NB)
     out_ref[...] = w_ref[block, :] - three(r_high[block, :], r_low[block, :], c_high[...], c_low[...])
@@ -650,20 +676,19 @@
 
 
 def update(matrix, *panels):
-    place = jnp.stack([lax.axis_index("prow"), lax.axis_index("pcol")]).astype(jnp.int32)
     vmem = pl.BlockSpec(memory_space=pltpu.VMEM)
     return pl.pallas_call(
         update_kernel,
         out_shape=jax.ShapeDtypeStruct((ROWS, COLS), F32),
         grid=(ROWS // NB,),
-        in_specs=[pl.BlockSpec(memory_space=pltpu.SMEM)] + [vmem] * 5,
+        in_specs=[vmem] * 5,
         out_specs=pl.BlockSpec((NB, COLS), lambda i: (i, 0)),
         compiler_params=pltpu.CompilerParams(vmem_limit_bytes=32 * 2**20),
         cost_estimate=pl.CostEstimate(
             flops=2 * 3 * ROWS * COLS * 2 * NB, bytes_accessed=2**24, transcendentals=0
         ),
         name="update",
-    )(place, matrix, *panels)
+    )(matrix, *panels)
 
 
 def body(matrix):

time: 81.5 us -> 78.3 us (0.961)
  the two profiles are of different devices: /device:TPU:65 before, /device:TPU:45 now
where the time goes in v5:
time: 78.3 us; the launch traced here: 77.6 us
  Pallas kernels  77.6 us (99%)
    pallas_call x1, Pallas kernels, make_panels(): pl.pallas_call(panels_kernel, out_shape=(jax.ShapeDtypeStruct((ROWS, COLS...  64.4 us
    pallas_call x1, Pallas kernels, update(): pl.pallas_call(update_kernel, out_shape=jax.ShapeDtypeStruct((ROWS, COLS)...  13.1 us

profile of v5, /device:TPU:45, one launch (start us, length us, event | category | flops | bytes accessed | tf_op | source)
XLA Modules:
  0.0 77.6 jit_solution(1007549287110466196)
XLA Ops:
  0.0 64.4 %panels.1 = (f32[2560,1280]{1,0:T(8,128)S(1)}, bf16[2560,512]{1,0:T(8,128)(2,1)S(1)}, bf16[2560,512]{1,0:T(8,128)(2,1)S(1)}, bf16[512,1280]{1,0:T(8,128)(2,1)S(1)}, bf16[512,1280]{1,0:T(8,128)(2,1)S(1)}) custom-call(f32[2560,1280]{1,0:T(8,128)} %a_ref.1), custom_call_target="tpu_custom_call" | custom-call | flops 1073741824 | bytes 16777216 | tf_op jit(solution)/shard_map/panels/pallas_call | solution.py:612
  64.5 13.1 %update.1 = f32[2560,1280]{1,0:T(8,128)} custom-call(f32[2560,1280]{1,0:T(8,128)S(1)} %get-tuple-element.10.w_ref, bf16[2560,512]{1,0:T(8,128)(2,1)S(1)} %get-tuple-element.11.r_high, bf16[2560,512]{1,0:T(8,128)(2,1)S(1)} %get-tuple-element.12.r_low, bf16[512,1280]{1,0:T(8,128)(2,1)S(1)} %get-tuple-element.13.c_high, ...), custom_call_target="tpu_custom_call" | custom-call | flops 10066329600 | bytes 16777216 | tf_op jit(solution)/shard_map/update/pallas_call | solution.py:680

commit v6 on v5

--- a/solution.py
+++ b/solution.py
@@ -19,7 +19,7 @@
 STRIPS = NB // STRIP
 BLOCKS = (3, 4, 3)
 FIRST_MESSAGE = (0, 3, 7)
-PLACES = (25, 27, 42)
+PLACES = (25, 27, 40)
 ITEMS = CHUNKS + len(PLACES)
 LAG = 4
 DEEPEST = 5
@@ -142,6 +142,9 @@
     return [n for n in range(16) if parents[neighbour(n, direction)] == n]
 
 
+(ROOT_GIVES,) = [d for d in range(4) if 0 in senders(1, 0, d)]
+
+
 def panels_kernel(
     a_ref, w_ref, r_high, r_low, c_high, c_low, rows, slab, fac, fac_split, rest, left, leading, made, stage, lead, inv, low,
     local_sem, row_send, row_recv, slab_send, slab_recv,
@@ -175,8 +178,8 @@
     def greet(target):
         pl.semaphore_signal(barrier, 1, device_id=target, device_id_type=MESH)
 
-    for axis in "xyz":
-        for step in (1, 2, 3):
+    for axis, steps in (("x", (1, 3)), ("y", (1, 3)), ("z", (1, 2, 3))):
+        for step in steps:
             greet(on_line(axis, step))
     greet(sibling)
 
@@ -190,8 +193,6 @@
         greet(root)
 
     extra = jnp.where(is_root, 1, 0) + jnp.where(jnp.logical_or(gives_lead[0], gives_lead[2]), 3, 0)
-    pl.semaphore_wait(barrier, 10 + extra)
-
     index = core * 16 + pcol
     gives = [[None] * 4 for _ in range(2)]
     for k in range(2):
@@ -208,6 +209,7 @@
             for n in range(16):
                 value = value + jnp.where(index == c * 16 + n, handled_at(c, k, n), 0)
         depths.append(value)
+    pl.semaphore_wait(barrier, 8 + extra)
     targets = (on_line("x", 1), on_line("x", 3), on_line("y", 1), on_line("y", 3))
 
     def row_copy(src, k, d, first, count):
@@ -402,7 +404,7 @@
             def one(i, carry):
                 @pl.when(i < CHUNKS)
                 def _():
-                    send_chunk(a_ref, 0, i)
+                    row_copy(a_ref, 0, ROOT_GIVES, i * CHUNK, CHUNK).start()
 
                 return carry
 
@@ -567,14 +569,11 @@
         c_high[NB:2 * NB, tile] = high
         c_low[NB:2 * NB, tile] = low_part
 
-    def second_rows(i, carry):
-        block = pl.ds(pl.multiple_of(i * 2 * NB, 2 * NB), 2 * NB)
+    for i in range(2):
+        block = pl.ds(i * ROWS // 2, ROWS // 2)
         high, low_part = split(three_t(*split(rest[block, :]), fac_split[2, 0], fac_split[2, 1]))
         r_high[block, NB:2 * NB] = high
         r_low[block, NB:2 * NB] = low_part
-        return carry
-
-    lax.fori_loop(0, ROW_BLOCKS // 2, second_rows, 0)
 
     own_block().wait()
 

time: 78.3 us -> 77.4 us (0.989)
  Pallas kernels: 77.6 us -> 76.7 us
    pallas_call x1, Pallas kernels: 64.4 us -> 63.5 us  [make_panels(): pl.pallas_call(panels_kernel, out_shape=(jax.ShapeDtypeStruct((ROWS, COLS...]
where the time goes in v6:
time: 77.4 us; the launch traced here: 76.7 us
  Pallas kernels  76.7 us (99%)
    pallas_call x1, Pallas kernels, make_panels(): pl.pallas_call(panels_kernel, out_shape=(jax.ShapeDtypeStruct((ROWS, COLS...  63.5 us
    pallas_call x1, Pallas kernels, update(): pl.pallas_call(update_kernel, out_shape=jax.ShapeDtypeStruct((ROWS, COLS)...  13.1 us

profile of v6, /device:TPU:45, one launch (start us, length us, event | category | flops | bytes accessed | tf_op | source)
XLA Modules:
  0.0 76.7 jit_solution(7169987850837710125)
XLA Ops:
  0.0 63.5 %panels.1 = (f32[2560,1280]{1,0:T(8,128)S(1)}, bf16[2560,512]{1,0:T(8,128)(2,1)S(1)}, bf16[2560,512]{1,0:T(8,128)(2,1)S(1)}, bf16[512,1280]{1,0:T(8,128)(2,1)S(1)}, bf16[512,1280]{1,0:T(8,128)(2,1)S(1)}) custom-call(f32[2560,1280]{1,0:T(8,128)} %a_ref.1), custom_call_target="tpu_custom_call" | custom-call | flops 1073741824 | bytes 16777216 | tf_op jit(solution)/shard_map/panels/pallas_call | solution.py:611
  63.5 13.1 %update.1 = f32[2560,1280]{1,0:T(8,128)} custom-call(f32[2560,1280]{1,0:T(8,128)S(1)} %get-tuple-element.10.w_ref, bf16[2560,512]{1,0:T(8,128)(2,1)S(1)} %get-tuple-element.11.r_high, bf16[2560,512]{1,0:T(8,128)(2,1)S(1)} %get-tuple-element.12.r_low, bf16[512,1280]{1,0:T(8,128)(2,1)S(1)} %get-tuple-element.13.c_high, ...), custom_call_target="tpu_custom_call" | custom-call | flops 10066329600 | bytes 16777216 | tf_op jit(solution)/shard_map/update/pallas_call | solution.py:679

commit v7 on v6

--- a/solution.py
+++ b/solution.py
@@ -30,6 +30,7 @@
 ROWS_WORK = TICKS - ROWS // NB
 COLUMN_BLOCKS = COLS // NB
 ROW_BLOCKS = ROWS // NB
+assert SLAB_TICK + LAG * DEEPEST + STRIPS <= FIRST_WORK == ROWS_WORK - COLUMN_BLOCKS
 AHEAD = 6
 PUMP = 5
 
@@ -348,7 +349,7 @@
         fac[span] = made[span]
         each_fac(part, 0, begin)
 
-    def pass_rows(tick):
+    def pass_rows(tick, parts):
         for k in range(2):
             n = tick - LAG * depths[k]
             skips = jnp.int32(0)
@@ -371,8 +372,8 @@
             def _(k=k, i=i):
                 send_chunk(a_ref, k, i)
 
-            for part, place in enumerate(PLACES):
-                now = both(n == place, core * 2 + k < BLOCKS[part])
+            for part in parts:
+                now = both(n == PLACES[part], core * 2 + k < BLOCKS[part])
                 if k == 0:
                     now = both(now, jnp.logical_not(is_root))
 
@@ -488,12 +489,12 @@
         def _(s=s):
             own_slab(s).wait()
 
-    def step(tick):
-        pass_rows(tick)
+    def late(tick):
+        pass_rows(tick, (2,))
+
+    def early(tick, carry):
+        pass_rows(tick, (0, 1, 2))
         pass_slab(tick)
-
-    def early(tick, carry):
-        step(tick)
 
         @pl.when(tick == OWN_TICK)
         def _():
@@ -512,7 +513,7 @@
         fac_split[part, 0], fac_split[part, 1] = split(fac[part])
 
     def first_columns(j, carry):
-        step(FIRST_WORK + j)
+        late(FIRST_WORK + j)
         tile = pl.ds(pl.multiple_of(j * NB, NB), NB)
         high, low_part = split(three(fac_split[0, 0], fac_split[0, 1], *split(slab[0, :, tile])))
         c_high[0:NB, tile] = high
@@ -521,7 +522,7 @@
         return carry
 
     def first_rows(i, carry):
-        step(ROWS_WORK + i)
+        late(ROWS_WORK + i)
         block = pl.ds(pl.multiple_of(i * NB, NB), NB)
         first = three_t(*split(rows[0, block, :]), fac_split[0, 0], fac_split[0, 1])
         high, low_part = split(first)
@@ -559,7 +560,6 @@
     part_here(0)
     part_here(1)
     lax.fori_loop(0, COLUMN_BLOCKS, first_columns, 0)
-    lax.fori_loop(FIRST_WORK + COLUMN_BLOCKS, ROWS_WORK, early, 0)
     lax.fori_loop(0, ROW_BLOCKS, first_rows, 0)
     part_here(2)
 

time: 77.4 us -> 75.8 us (0.979)
  Pallas kernels: 76.7 us -> 74.8 us
    pallas_call x1, Pallas kernels: 63.5 us -> 61.7 us  [make_panels(): pl.pallas_call(panels_kernel, out_shape=(jax.ShapeDtypeStruct((ROWS, COLS...]
where the time goes in v7:
time: 75.8 us; the launch traced here: 74.8 us
  Pallas kernels  74.8 us (99%)
    pallas_call x1, Pallas kernels, make_panels(): pl.pallas_call(panels_kernel, out_shape=(jax.ShapeDtypeStruct((ROWS, COLS...  61.7 us
    pallas_call x1, Pallas kernels, update(): pl.pallas_call(update_kernel, out_shape=jax.ShapeDtypeStruct((ROWS, COLS)...  13.1 us

profile of v7, /device:TPU:45, one launch (start us, length us, event | category | flops | bytes accessed | tf_op | source)
XLA Modules:
  0.0 74.8 jit_solution(1878232395731270778)
XLA Ops:
  0.0 61.7 %panels.1 = (f32[2560,1280]{1,0:T(8,128)S(1)}, bf16[2560,512]{1,0:T(8,128)(2,1)S(1)}, bf16[2560,512]{1,0:T(8,128)(2,1)S(1)}, bf16[512,1280]{1,0:T(8,128)(2,1)S(1)}, bf16[512,1280]{1,0:T(8,128)(2,1)S(1)}) custom-call(f32[2560,1280]{1,0:T(8,128)} %a_ref.1), custom_call_target="tpu_custom_call" | custom-call | flops 1073741824 | bytes 16777216 | tf_op jit(solution)/shard_map/panels/pallas_call | solution.py:611
  61.7 13.1 %update.1 = f32[2560,1280]{1,0:T(8,128)} custom-call(f32[2560,1280]{1,0:T(8,128)S(1)} %get-tuple-element.10.w_ref, bf16[2560,512]{1,0:T(8,128)(2,1)S(1)} %get-tuple-element.11.r_high, bf16[2560,512]{1,0:T(8,128)(2,1)S(1)} %get-tuple-element.12.r_low, bf16[512,1280]{1,0:T(8,128)(2,1)S(1)} %get-tuple-element.13.c_high, ...), custom_call_target="tpu_custom_call" | custom-call | flops 10066329600 | bytes 16777216 | tf_op jit(solution)/shard_map/update/pallas_call | solution.py:679

commit v8 on v7

--- a/solution.py
+++ b/solution.py
@@ -24,13 +24,14 @@
 LAG = 4
 DEEPEST = 5
 TICKS = ITEMS + LAG * DEEPEST
-SLAB_TICK = 12
+SLAB_TICK = 7
+SLAB_TICKS = STRIPS * 4 // 3
 OWN_TICK = 44
 FIRST_WORK = PLACES[1] + LAG * DEEPEST + 1
 ROWS_WORK = TICKS - ROWS // NB
 COLUMN_BLOCKS = COLS // NB
 ROW_BLOCKS = ROWS // NB
-assert SLAB_TICK + LAG * DEEPEST + STRIPS <= FIRST_WORK == ROWS_WORK - COLUMN_BLOCKS
+assert SLAB_TICK + LAG * DEEPEST + SLAB_TICKS <= FIRST_WORK == ROWS_WORK - COLUMN_BLOCKS
 AHEAD = 6
 PUMP = 5
 
@@ -349,14 +350,19 @@
         fac[span] = made[span]
         each_fac(part, 0, begin)
 
-    def pass_rows(tick, parts):
+    def pass_rows(tick, begin_tick, end_tick):
+        parts = [
+            part for part, place in enumerate(PLACES)
+            if begin_tick - LAG * DEEPEST <= place < end_tick
+        ]
+        passed = sum(place < begin_tick - LAG * DEEPEST for place in PLACES)
         for k in range(2):
             n = tick - LAG * depths[k]
-            skips = jnp.int32(0)
+            skips = jnp.int32(passed)
             special = n < 0
-            for place in PLACES:
-                skips = skips + jnp.where(n > place, 1, 0)
-                special = jnp.logical_or(special, n == place)
+            for part in parts:
+                skips = skips + jnp.where(n > PLACES[part], 1, 0)
+                special = jnp.logical_or(special, n == PLACES[part])
             i = n - skips
             here = both(jnp.logical_not(special), n < ITEMS)
             mine = both(here, pcol == k)
@@ -384,15 +390,18 @@
 
     def pass_slab(tick):
         for s in range(2):
-            j = tick - SLAB_TICK - LAG * slab_depths[s]
-            here = both(j >= 0, j < STRIPS)
+            turn = (tick - SLAB_TICK - LAG * slab_depths[s]) * 3
+            j = turn // 4
+            here = both(both(turn >= 0, turn % 4 < 3), j < STRIPS)
 
             @pl.when(both(here, prow != s))
             def _(s=s, j=j):
                 slab_copy(None, s, 0, j * STRIP, STRIP).wait_recv()
                 send_strip(None, s, j)
 
-            @pl.when(both(both(tick < STRIPS, prow == s), jnp.logical_not(is_root)))
+    def source_slab(tick):
+        for s in range(2):
+            @pl.when(both(prow == s, jnp.logical_not(is_root)))
             def _(s=s):
                 send_strip(a_ref, s, tick)
 
@@ -489,18 +498,19 @@
         def _(s=s):
             own_slab(s).wait()
 
+    def ticks(begin_tick, end_tick, sends, passes):
+        def one(tick, carry):
+            pass_rows(tick, begin_tick, end_tick)
+            if passes:
+                pass_slab(tick)
+            if sends:
+                source_slab(tick)
+            return carry
+
+        lax.fori_loop(begin_tick, end_tick, one, 0)
+
     def late(tick):
-        pass_rows(tick, (2,))
-
-    def early(tick, carry):
-        pass_rows(tick, (0, 1, 2))
-        pass_slab(tick)
-
-        @pl.when(tick == OWN_TICK)
-        def _():
-            own_block().start()
-
-        return carry
+        pass_rows(tick, FIRST_WORK, TICKS)
 
     def part_here(part):
         for k in range(2):
@@ -533,7 +543,12 @@
 
     @pl.when(jnp.logical_not(is_root))
     def _():
-        lax.fori_loop(0, FIRST_WORK, early, 0)
+        ticks(0, SLAB_TICK + LAG, True, False)
+        ticks(SLAB_TICK + LAG, STRIPS, True, True)
+        ticks(STRIPS, PLACES[0], False, True)
+        ticks(PLACES[0], OWN_TICK, False, True)
+        own_block().start()
+        ticks(OWN_TICK, FIRST_WORK, False, True)
 
     @pl.when(is_root)
     def _():

time: 75.8 us -> 78.8 us (1.040)
  Pallas kernels: 74.8 us -> 77.7 us
    pallas_call x1, Pallas kernels: 61.7 us -> 64.6 us  [make_panels(): pl.pallas_call(panels_kernel, out_shape=(jax.ShapeDtypeStruct((ROWS, COLS...]
where the time goes in v8:
time: 78.8 us; the launch traced here: 77.7 us
  Pallas kernels  77.7 us (99%)
    pallas_call x1, Pallas kernels, make_panels(): pl.pallas_call(panels_kernel, out_shape=(jax.ShapeDtypeStruct((ROWS, COLS...  64.6 us
    pallas_call x1, Pallas kernels, update(): pl.pallas_call(update_kernel, out_shape=jax.ShapeDtypeStruct((ROWS, COLS)...  13.1 us

profile of v8, /device:TPU:45, one launch (start us, length us, event | category | flops | bytes accessed | tf_op | source)
XLA Modules:
  0.0 77.7 jit_solution(13606796370349915376)
XLA Ops:
  0.0 64.6 %panels.1 = (f32[2560,1280]{1,0:T(8,128)S(1)}, bf16[2560,512]{1,0:T(8,128)(2,1)S(1)}, bf16[2560,512]{1,0:T(8,128)(2,1)S(1)}, bf16[512,1280]{1,0:T(8,128)(2,1)S(1)}, bf16[512,1280]{1,0:T(8,128)(2,1)S(1)}) custom-call(f32[2560,1280]{1,0:T(8,128)} %a_ref.1), custom_call_target="tpu_custom_call" | custom-call | flops 1073741824 | bytes 16777216 | tf_op jit(solution)/shard_map/panels/pallas_call | solution.py:626
  64.6 13.1 %update.1 = f32[2560,1280]{1,0:T(8,128)} custom-call(f32[2560,1280]{1,0:T(8,128)S(1)} %get-tuple-element.10.w_ref, bf16[2560,512]{1,0:T(8,128)(2,1)S(1)} %get-tuple-element.11.r_high, bf16[2560,512]{1,0:T(8,128)(2,1)S(1)} %get-tuple-element.12.r_low, bf16[512,1280]{1,0:T(8,128)(2,1)S(1)} %get-tuple-element.13.c_high, ...), custom_call_target="tpu_custom_call" | custom-call | flops 10066329600 | bytes 16777216 | tf_op jit(solution)/shard_map/update/pallas_call | solution.py:694
